TPU v7x, 128 devices: a whole 4x4x4 slice. The times are simulated.
128 devices in a mesh: section: 2 (over x_hi), fsdp: 32 (over y, z, x_lo), ctx: 2 (over core).
Axes of the slice: x: 4 (x_hi: 2, x_lo: 2; x = x_hi * 2 + x_lo), y: 4, z: 4, core: 2. Of those that a mesh axis runs over, the one named last changes fastest.
Arguments:
- tokens: bfloat16 [2, 4096, 960], P(None, ('fsdp', 'ctx')), may hold values from -6 to 6
- segments: int32 [2, 4096], P(None, 'fsdp'), may hold values from 0 to 4, as said below
- gain_attn: bfloat16 [2, 960], P('section', 'fsdp'), may hold values from 0.5 to 1.5
- w_qkv: bfloat16 [2, 960, 1600], P('section', 'fsdp'), may hold values from -0.1875 to 0.1875
- w_out: bfloat16 [2, 960, 960], P('section', 'fsdp'), may hold values from -0.75 to 0.75
- gain_ffn: bfloat16 [2, 960], P('section', 'fsdp'), may hold values from 0.5 to 1.5
- w_gu: bfloat16 [2, 960, 5120], P('section', 'fsdp'), may hold values from -0.1875 to 0.1875
- w_down: bfloat16 [2, 960, 2560], P('section', 'fsdp'), may hold values from -0.25 to 0.25
- d_out: bfloat16 [2, 4096, 960], P(None, ('fsdp', 'ctx')), may hold values from -6 to 6
Outputs:
- acts: bfloat16 [2, 2, 4096, 960], P('section', None, ('fsdp', 'ctx'))
- input_grad: bfloat16 [2, 2, 4096, 960], P('section', None, ('fsdp', 'ctx'))
- grad_gain_attn: float32 [2, 960], P('section', 'fsdp')
- grad_qkv: float32 [2, 960, 1600], P('section', 'fsdp')
- grad_out: float32 [2, 960, 960], P('section', 'fsdp')
- grad_gain_ffn: float32 [2, 960], P('section', 'fsdp')
- grad_gu: float32 [2, 960, 5120], P('section', 'fsdp')
- grad_down: float32 [2, 960, 2560], P('section', 'fsdp')
Inputs may be any that keep to these rules, and one draw needn't show every extreme that they name: `segments`: within each sequence of 128 tokens the segment numbers start at 0, never fall, and end at 4.
All inputs are finite; a program needn't handle non-finite values.
Results may differ from a plain program's by a relative error of at most 0.034.
Values may be sent and summed in bfloat16 or wider, within the bound.
A program may use at most 256 MiB of HBM per device.

v0:
```python
import math

import jax
import jax.numpy as jnp
from jax import lax
from jax.sharding import PartitionSpec as P

HEADS = 15
KV_HEADS = 5
HEAD = 64


norm_eps = 1e-05
rope_base = 100000.0


def from_behind(block, axis, distance):
    devices = range(lax.axis_size(axis))
    route = [(i - distance, i) for i in devices if i - distance in devices]
    return lax.ppermute(block, axis, route)


def side_by_side(arrays, axis, dim, along):
    widths = [math.prod(a.shape[along:]) for a in arrays]
    both = jnp.concatenate(
        [a.reshape(*a.shape[:along], w) for a, w in zip(arrays, widths)], axis=along
    )
    filled = lax.all_gather(both, axis, axis=dim, tiled=True)
    parts = jnp.split(filled, [sum(widths[:k]) for k in range(1, len(widths))], axis=along)
    return tuple(
        (b.reshape(*filled.shape[:along], *a.shape[along:]) for a, b in zip(arrays, parts))
    )


def frequencies():
    return jnp.power(
        jnp.float32(rope_base), -jnp.arange(HEAD // 2, dtype=jnp.float32) * (2.0 / HEAD)
    )


def rotate(vector, cosine, sine_part):
    half_width = vector.shape[-1] // 2
    first_half, second_half = (vector[..., :half_width], vector[..., half_width:])
    return jnp.concatenate(
        [
            first_half * cosine - second_half * sine_part,
            second_half * cosine + first_half * sine_part,
        ],
        axis=-1,
    )


def unrotate(grad_vec, cosine, sine_part):
    half_width = grad_vec.shape[-1] // 2
    first_half, second_half = (grad_vec[..., :half_width], grad_vec[..., half_width:])
    return jnp.concatenate(
        [
            first_half * cosine + second_half * sine_part,
            second_half * cosine - first_half * sine_part,
        ],
        axis=-1,
    )


def norm_stats(values):
    inverse = lax.rsqrt(jnp.mean(values * values, axis=-1, keepdims=True) + norm_eps)
    return (values * inverse, inverse)


def norm_back(d_normal, normal, inverse):
    return inverse * (d_normal - normal * jnp.mean(normal * d_normal, axis=-1, keepdims=True))


def right_product(left_side, weight_piece):
    return lax.dot_general(
        left_side, weight_piece, (((1,), (1,)), ((), ())), preferred_element_type=jnp.float32
    )


def gained_product(left_side, pieces):
    gain_piece, weight_piece = pieces
    product = lax.dot_general(
        left_side, weight_piece, (((1,), (1,)), ((), ())), preferred_element_type=jnp.float32
    )
    return product * gain_piece.astype(jnp.float32)[None, :]


def held_scaled(normal, gain_full, weight_full):
    scaled = (normal * gain_full.astype(jnp.float32)[None, :]).astype(jnp.bfloat16)
    return (jnp.dot(scaled, weight_full, preferred_element_type=jnp.float32), scaled)


def attention_layout(seg_row, ctx_index, local_rows):
    full_len = seg_row.shape[0]
    earlier = jnp.sum((seg_row[None, :] < seg_row[:, None]).astype(jnp.int32), axis=1)
    position = jnp.arange(full_len, dtype=jnp.int32) - earlier
    begin = ctx_index * local_rows
    before = jnp.maximum(ctx_index - 1, 0) * local_rows
    query_seg = lax.dynamic_slice_in_dim(seg_row, begin, local_rows)
    query_pos = lax.dynamic_slice_in_dim(position, begin, local_rows)
    key_seg = jnp.concatenate([lax.dynamic_slice_in_dim(seg_row, before, local_rows), query_seg])
    counter = jnp.arange(local_rows, dtype=jnp.int32)
    query_at = begin + counter
    key_at = jnp.concatenate([before + counter, query_at])
    prev_ok = jnp.concatenate(
        [jnp.full((local_rows,), ctx_index > 0), jnp.full((local_rows,), True)]
    )
    allowed = (
        (key_seg[None, :] == query_seg[:, None])
        & (key_at[None, :] <= query_at[:, None])
        & prev_ok[None, :]
    )
    angles = query_pos.astype(jnp.float32)[:, None] * frequencies()[None, :]
    return (allowed, jnp.cos(angles), jnp.sin(angles))


def masked_scores(query_rows, gathered_key_rows, allowed):
    scores = jnp.einsum(
        "obun,qbn->buoq", query_rows, gathered_key_rows, preferred_element_type=jnp.float32
    ) * HEAD ** (-0.5)
    return jnp.where(allowed[None, None], scores, -1e30)


def forward_layer(inputs, layout, params):
    allowed, cosine, sine_part = layout
    gain_one, weight_qkv, weight_out, gain_two, weight_gu, weight_down = params
    local_rows = inputs.shape[0]
    group_size = HEADS // KV_HEADS
    query_width = HEADS * HEAD
    kv_width = KV_HEADS * HEAD
    normal_one, inverse_one = norm_stats(inputs)
    qkv, normed_one = held_scaled(normal_one, gain_one, weight_qkv)
    query_rows = rotate(
        qkv[:, :query_width].reshape(local_rows, KV_HEADS, group_size, HEAD),
        cosine[:, None, None, :],
        sine_part[:, None, None, :],
    ).astype(jnp.bfloat16)
    key_own = rotate(
        qkv[:, query_width : query_width + kv_width].reshape(local_rows, KV_HEADS, HEAD),
        cosine[:, None, :],
        sine_part[:, None, :],
    ).astype(jnp.bfloat16)
    value_own = (
        qkv[:, query_width + kv_width :].reshape(local_rows, KV_HEADS, HEAD).astype(jnp.bfloat16)
    )
    key_prev, value_prev = from_behind((key_own, value_own), "ctx", 1)
    gathered_key_rows = jnp.concatenate([key_prev, key_own], axis=0)
    gathered_value_rows = jnp.concatenate([value_prev, value_own], axis=0)
    scores = masked_scores(query_rows, gathered_key_rows, allowed)
    row_peak = jnp.max(scores, axis=-1, keepdims=True)
    exponent = jnp.exp(scores - row_peak)
    row_total = jnp.sum(exponent, axis=-1, keepdims=True)
    reduced_probabilities = (exponent / row_total).astype(jnp.bfloat16)
    log_total = row_peak + jnp.log(row_total)
    attended = jnp.einsum(
        "fcuy,yfo->ufco",
        reduced_probabilities,
        gathered_value_rows,
        preferred_element_type=jnp.float32,
    )
    attended = attended.reshape(local_rows, query_width).astype(jnp.bfloat16)
    branch = right_product(attended, weight_out)
    hidden = inputs + branch
    normal_two, inverse_two = norm_stats(hidden)
    gate_up, normed_two = held_scaled(normal_two, gain_two, weight_gu)
    half_width = gate_up.shape[1] // 2
    gate_in = gate_up[:, :half_width]
    upper = gate_up[:, half_width:]
    mixed = (jax.nn.silu(gate_in) * upper).astype(jnp.bfloat16)
    result = right_product(mixed, weight_down)
    record = (
        normal_one,
        inverse_one,
        normed_one,
        query_rows,
        gathered_key_rows,
        gathered_value_rows,
        log_total,
        attended,
        normal_two,
        inverse_two,
        normed_two,
        gate_in,
        upper,
        mixed,
        allowed,
        cosine,
        sine_part,
    )
    return (hidden + result, record)


def backward_layer(d_output, record, params):
    (
        normal_one,
        inverse_one,
        normed_one,
        query_rows,
        gathered_key_rows,
        gathered_value_rows,
        log_total,
        attended,
        normal_two,
        inverse_two,
        normed_two,
        gate_in,
        upper,
        mixed,
        allowed,
        cosine,
        sine_part,
    ) = record
    gain_one, weight_qkv, weight_out, gain_two, weight_gu, weight_down = params
    local_rows = d_output.shape[0]
    group_size = HEADS // KV_HEADS
    query_width = HEADS * HEAD
    kv_width = KV_HEADS * HEAD
    d_result = d_output.astype(jnp.bfloat16)
    d_mixed = jnp.dot(d_result, weight_down, preferred_element_type=jnp.float32)
    sigmoid_gate = jax.nn.sigmoid(gate_in)
    d_gate = d_mixed * upper * sigmoid_gate * (1.0 + gate_in * (1.0 - sigmoid_gate))
    d_upper = d_mixed * gate_in * sigmoid_gate
    d_gate_up = jnp.concatenate([d_gate, d_upper], axis=1).astype(jnp.bfloat16)
    d_normal_two = gained_product(d_gate_up, (gain_two, weight_gu))
    d_hidden = d_output + norm_back(d_normal_two, normal_two, inverse_two)
    d_branch = d_hidden.astype(jnp.bfloat16)
    d_attended = jnp.dot(d_branch, weight_out, preferred_element_type=jnp.float32)
    attention_gradient = d_attended.astype(jnp.bfloat16).reshape(
        local_rows, KV_HEADS, group_size, HEAD
    )
    scores = masked_scores(query_rows, gathered_key_rows, allowed)
    probs = jnp.exp(scores - log_total)
    reduced_probabilities = probs.astype(jnp.bfloat16)
    probability_gradient = jnp.einsum(
        "obun,qbn->buoq",
        attention_gradient,
        gathered_value_rows,
        preferred_element_type=jnp.float32,
    )
    row_dot = jnp.sum(probability_gradient * probs, axis=-1, keepdims=True)
    score_gradient = (probs * (probability_gradient - row_dot)).astype(jnp.bfloat16)
    d_queries = jnp.einsum(
        "fcuy,yfo->ufco", score_gradient, gathered_key_rows, preferred_element_type=jnp.float32
    ) * HEAD ** (-0.5)
    d_keys = jnp.einsum(
        "vmil,ivmj->lvj", score_gradient, query_rows, preferred_element_type=jnp.float32
    ) * HEAD ** (-0.5)
    value_rows_gradient = jnp.einsum(
        "vmil,ivmj->lvj",
        reduced_probabilities,
        attention_gradient,
        preferred_element_type=jnp.float32,
    )
    back_key, back_value = (
        from_behind(d_keys[:local_rows].astype(jnp.bfloat16), "ctx", -1).astype(jnp.float32),
        from_behind(value_rows_gradient[:local_rows].astype(jnp.bfloat16), "ctx", -1).astype(
            jnp.float32
        ),
    )
    d_key = d_keys[local_rows:] + back_key
    d_value = value_rows_gradient[local_rows:] + back_value
    d_qkv = jnp.concatenate(
        [
            unrotate(d_queries, cosine[:, None, None, :], sine_part[:, None, None, :]).reshape(
                local_rows, query_width
            ),
            unrotate(d_key, cosine[:, None, :], sine_part[:, None, :]).reshape(
                local_rows, kv_width
            ),
            d_value.reshape(local_rows, kv_width),
        ],
        axis=1,
    ).astype(jnp.bfloat16)
    d_normal_one = gained_product(d_qkv, (gain_one, weight_qkv))
    d_inputs = d_hidden + norm_back(d_normal_one, normal_one, inverse_one)
    pairs = ((normed_one, d_qkv), (d_branch, attended), (normed_two, d_gate_up), (d_result, mixed))
    return (d_inputs, pairs)


def reduce_grads(pair_groups):
    blocks = []
    for member in range(4):
        summed = None
        for pairs in pair_groups:
            left_side, right_side = pairs[member]
            product = lax.dot_general(
                left_side, right_side, (((0,), (0,)), ((), ())), preferred_element_type=jnp.float32
            )
            summed = product if summed is None else summed + product
        blocks.append(summed)
    return lax.psum_scatter(
        jnp.concatenate(blocks, axis=1).astype(jnp.bfloat16),
        "fsdp",
        scatter_dimension=0,
        tiled=True,
    ).astype(jnp.float32)


def per_device(tokens, segments, gain_attn, w_qkv, w_out, gain_ffn, w_gu, w_down, d_out):
    section_idx = lax.axis_index("section")
    ctx_index = lax.axis_index("ctx")
    micro_count = tokens.shape[0]
    local_rows = tokens.shape[1]
    fwd_params = side_by_side(
        (gain_attn[0], w_qkv[0], w_out[0], gain_ffn[0], w_gu[0], w_down[0]), "fsdp", 0, 1
    )
    is_first = section_idx == 0
    records = []
    section_out = []
    received = jnp.zeros(tokens.shape[1:], jnp.bfloat16)
    for tick in range(micro_count + 1):
        own_batch = min(tick, micro_count - 1)
        prior_batch = max(tick - 1, 0)
        seg_row = jnp.where(is_first, segments[own_batch], segments[prior_batch])
        layout = attention_layout(seg_row, ctx_index, local_rows)
        own_input = tokens[tick] if tick < micro_count else jnp.zeros_like(tokens[0])
        inputs = jnp.where(is_first, own_input, received).astype(jnp.float32)
        result, record = forward_layer(inputs, layout, fwd_params)
        result = result.astype(jnp.bfloat16)
        section_out.append(result)
        records.append(record)
        if tick < micro_count:
            received = from_behind(result, "section", 1)
    acts = jnp.stack(
        [
            jnp.where(is_first, section_out[batch], section_out[batch + 1])
            for batch in range(micro_count)
        ]
    )
    bwd_params = side_by_side(
        (gain_attn[0], w_qkv[0], w_out[0], gain_ffn[0], w_gu[0], w_down[0]), "fsdp", 0, 1
    )
    grad_list = []
    pair_list = []
    summed_rows = None
    arriving = jnp.zeros(tokens.shape[1:], jnp.bfloat16)
    for tick in range(micro_count + 1):
        record = records[micro_count - tick]
        last_grad = (
            d_out[micro_count - 1 - tick] if tick < micro_count else jnp.zeros_like(d_out[0])
        )
        d_output = jnp.where(is_first, arriving, last_grad).astype(jnp.float32)
        d_inputs, pairs = backward_layer(d_output, record, bwd_params)
        d_inputs = d_inputs.astype(jnp.bfloat16)
        grad_list.append(d_inputs)
        if tick < micro_count:
            arriving = from_behind(d_inputs, "section", -1)
        pair_list.append(pairs)
    summed_rows = reduce_grads(pair_list)
    input_grad = jnp.stack(
        [
            jnp.where(is_first, grad_list[micro_count - batch], grad_list[micro_count - 1 - batch])
            for batch in range(micro_count)
        ]
    )
    summed_rows = lax.psum(summed_rows.astype(jnp.bfloat16), "ctx").astype(jnp.float32)
    qkv_cols = w_qkv.shape[2]
    out_cols = w_out.shape[2]
    gu_cols = w_gu.shape[2]
    grad_qkv = summed_rows[:, :qkv_cols]
    grad_out = summed_rows[:, qkv_cols : qkv_cols + out_cols]
    grad_gu = summed_rows[:, qkv_cols + out_cols : qkv_cols + out_cols + gu_cols]
    grad_down = summed_rows[:, qkv_cols + out_cols + gu_cols :]
    grad_gain_attn = jnp.sum(grad_qkv * w_qkv[0].astype(jnp.float32), axis=1) / gain_attn[0].astype(
        jnp.float32
    )
    grad_gain_ffn = jnp.sum(grad_gu * w_gu[0].astype(jnp.float32), axis=1) / gain_ffn[0].astype(
        jnp.float32
    )
    return (
        acts[None],
        input_grad[None],
        grad_gain_attn[None],
        grad_qkv[None],
        grad_out[None],
        grad_gain_ffn[None],
        grad_gu[None],
        grad_down[None],
    )


def solution(mesh):
    in_specs = (
        P(None, ("fsdp", "ctx"), None),
        P(None, "fsdp"),
        P("section", "fsdp"),
        P("section", "fsdp", None),
        P("section", "fsdp", None),
        P("section", "fsdp"),
        P("section", "fsdp", None),
        P("section", "fsdp", None),
        P(None, ("fsdp", "ctx"), None),
    )
    out_specs = (
        P("section", None, ("fsdp", "ctx"), None),
        P("section", None, ("fsdp", "ctx"), None),
        P("section", "fsdp"),
        P("section", "fsdp", None),
        P("section", "fsdp", None),
        P("section", "fsdp"),
        P("section", "fsdp", None),
        P("section", "fsdp", None),
    )
    return jax.shard_map(
        per_device, mesh=mesh, in_specs=in_specs, out_specs=out_specs, check_vma=False
    )
```

profile of v0, /device:TPU:1, one launch (start us, length us, event | category | flops | bytes accessed | tf_op | source)
XLA Modules:
  0.0 1312.0 jit_solution(12134811460420728837)
XLA Ops:
  19.5 450.6 %all-gather.3.cloned.1.call-done = bf16[32,30,10242]{2,1,0:T(8,128)(2,1)} async-done(((bf16[1,30,10242]{2,1,0:T(8,128)(2,1)}), bf16[32,30,10242]{2,1,0:T(8,128)(2,1)}) %all-gather.3.cloned.1.call-update) | async-done | bytes 19664656 | tf_op jit(solution)/shard_map/all_gather | solution.py:28
  470.1 19.9 %reshape.751 = bf16[960,10242]{1,0:T(8,128)(2,1)} reshape(bf16[32,30,10242]{2,1,0:T(8,128)(2,1)} %all-gather.3.cloned.1.call-done) | data formatting | bytes 39329280
  503.6 7.2 fusion.11
  511.1 4.8 fusion.79
  535.4 7.2 fusion.9
  548.1 5.6 collective-permute-start.5
  574.0 7.2 fusion.7
  581.2 5.1 multiply_convert_fusion.5
  586.3 7.8 multiply_reduce_fusion.6
  600.2 8.2 fusion.104
  611.2 4.6 collective-permute-start.9
  623.0 5.1 fusion.151
  646.5 7.9 multiply_reduce_fusion.5
  659.6 8.1 fusion.103
  667.8 5.3 fusion.221
  698.5 8.0 multiply_reduce_fusion.4
  721.5 17.7 %add_convert_fusion = bf16[960,5120]{1,0:T(8,128)(2,1)} fusion(f32[960,5120]{1,0:T(8,128)} %fusion.104, f32[960,5120]{1,0:T(8,128)} %fusion.103, bf16[64,2560]{1,0:T(8,128)(2,1)S(1)} %copy-done.38, bf16[64,2560]{1,0:T(8,128)(2,1)S(1)} %copy-done.36, f32[64,960]{1,0:T(8,128)S(1)} %copy-done.19, f32[960]{0:T(1024)S(1)} %get-tuple-element.48, f32[64]{0:T(128)S(1)} %copy-done.94), kind=kOutput, calls=%fused_computation | convolution fusion | flops 645386240 | bytes 50057216 | tf_op jit(solution)/shard_map/dot_general | solution.py:286
  739.3 10.3 add_convert_fusion.1
  751.9 6.0 add_convert_fusion.2
  757.9 28.5 %concatenate.147 = bf16[960,10240]{1,0:T(8,128)(2,1)} concatenate(bf16[960,1600]{1,0:T(8,128)(2,1)S(1)} %add_convert_fusion.2, bf16[960,960]{1,0:T(8,128)(2,1)} %add_convert_fusion.3, bf16[960,5120]{1,0:T(8,128)(2,1)} %add_convert_fusion, bf16[960,2560]{1,0:T(8,128)(2,1)} %add_convert_fusion.1), dimensions={1} | concatenate | bytes 39321600 | tf_op jit(solution)/shard_map/concatenate | solution.py:292
  786.5 445.7 %fusion = bf16[32,10240]{1,0:T(8,128)(2,1)S(1)} fusion(bf16[960,10240]{1,0:T(8,128)(2,1)} %concatenate.147), kind=kCustom, calls=%all-reduce-scatter | all-reduce-scatter fusion | flops 10485761 | bytes 20316672
  1241.3 20.1 %collective-permute-done.17 = bf16[30,10240]{1,0:T(8,128)(2,1)S(1)} collective-permute-done((bf16[30,10240]{1,0:T(8,128)(2,1)S(1)}, bf16[30,10240]{1,0:T(8,128)(2,1)S(1)}, u32[]{:S(2)}, u32[]{:S(2)}) %collective-permute-start.17) | collective-permute-done | bytes 614432
  1262.3 8.8 concatenate.148
  1278.6 18.5 %all-reduce.5.cloned.1.call-done = bf16[30,10240]{1,0:T(8,128)(2,1)} async-done(((bf16[30,10240]{1,0:T(8,128)(2,1)}), bf16[30,10240]{1,0:T(8,128)(2,1)}) %all-reduce.5.cloned.1.call-update) | async-done | bytes 614416 | tf_op jit(solution)/shard_map/psum | solution.py:356
  (418 shorter events, 176.6 us)
Async XLA Ops:
  7.2 462.9 %all-gather.3.cloned.1.call-start = ((), (), s32[]{:S(2)}) async-start(), calls=%async_computation.1 | async-start | bytes 21897216 | tf_op jit(solution)/shard_map/all_gather | solution.py:28
  11.1 1286.1 %all-reduce.5.cloned.1.call-start = ((), (), s32[]{:S(2)}) async-start(), calls=%async_computation | async-start | bytes 1310720 | tf_op jit(solution)/shard_map/psum | solution.py:356
  13.7 513.3 %copy-start.62 = (f32[64,32]{0,1:T(8,128)}, f32[64,32]{0,1:T(8,128)S(1)}, u32[]{:S(2)}) copy-start(f32[64,32]{0,1:T(8,128)S(1)} %get-tuple-element.109) | copy-start | bytes 24580
  13.7 548.2 %copy-start.66 = (f32[64,32]{0,1:T(8,128)}, f32[64,32]{0,1:T(8,128)S(1)}, u32[]{:S(2)}) copy-start(f32[64,32]{0,1:T(8,128)S(1)} %get-tuple-element.98) | copy-start | bytes 24580
  13.9 516.1 %copy-start.54 = (f32[64,32]{1,0:T(8,128)}, f32[64,32]{1,0:T(8,128)S(1)}, u32[]{:S(2)}) copy-start(f32[64,32]{1,0:T(8,128)S(1)} %copy.200) | copy-start | bytes 24580
  14.0 516.0 %copy-start.56 = (f32[64,32]{1,0:T(8,128)}, f32[64,32]{1,0:T(8,128)S(1)}, u32[]{:S(2)}) copy-start(f32[64,32]{1,0:T(8,128)S(1)} %copy.198) | copy-start | bytes 24580
  495.6 3.2 collective-permute-start.1
  497.0 3.2 collective-permute-start
  515.9 6.8 collective-permute-start.2
  527.1 3.4 collective-permute-start.4
  528.5 3.4 collective-permute-start.3
  548.1 7.9 collective-permute-start.5
  562.6 4.7 collective-permute-start.7
  564.6 5.1 collective-permute-start.6
  611.2 18.3 %collective-permute-start.9 = (bf16[64,5,64]{0,2,1:T(8,128)(2,1)}, bf16[64,5,64]{0,2,1:T(8,128)(2,1)}, u32[]{:S(2)}, u32[]{:S(2)}) collective-permute-start(bf16[64,5,64]{0,2,1:T(8,128)(2,1)} %slice.427), channel_id=1, source_target_pairs={{1,0},{3,2},{5,4},{7,6},{9,8},{11,10},{13,12},{15,14},{17,16},{19,... | collective-permute-start | bytes 122888 | tf_op jit(solution)/shard_map/ppermute | solution.py:20
  618.7 9.7 collective-permute-start.8
  634.5 7.5 collective-permute-start.10
  674.3 6.3 collective-permute-start.12
  677.8 2.6 collective-permute-start.11
  685.4 8.6 collective-permute-start.13
  710.3 40.5 %collective-permute-start.15 = (bf16[64,5,64]{0,2,1:T(8,128)(2,1)}, bf16[64,5,64]{0,2,1:T(8,128)(2,1)}, u32[]{:S(2)}, u32[]{:S(2)}) collective-permute-start(bf16[64,5,64]{0,2,1:T(8,128)(2,1)} %slice.423), channel_id=1, source_target_pairs={{1,0},{3,2},{5,4},{7,6},{9,8},{11,10},{13,12},{15,14},{17,16},{19,... | collective-permute-start | bytes 122888 | tf_op jit(solution)/shard_map/ppermute | solution.py:20
  715.0 35.6 %collective-permute-start.14 = (bf16[64,5,64]{0,2,1:T(8,128)(2,1)S(1)}, bf16[64,5,64]{0,2,1:T(8,128)(2,1)S(1)}, u32[]{:S(2)}, u32[]{:S(2)}) collective-permute-start(bf16[64,5,64]{0,2,1:T(8,128)(2,1)S(1)} %slice.424), channel_id=1, source_target_pairs={{1,0},{3,2},{5,4},{7,6},{9,8},{11,10},{13,12},{15,14},{17,16},{19,... | collective-permute-start | bytes 122888 | tf_op jit(solution)/shard_map/ppermute | solution.py:20
  1232.3 29.9 %collective-permute-start.16 = (bf16[32,10240]{1,0:T(8,128)(2,1)S(1)}, bf16[32,10240]{1,0:T(8,128)(2,1)}, u32[]{:S(2)}, u32[]{:S(2)}) collective-permute-start(bf16[32,10240]{1,0:T(8,128)(2,1)S(1)} %fusion), channel_id=1, source_target_pairs={{0,2},{2,4},{4,6},{6,8},{8,10},{10,12},{12,14},{14,16},{16,18},{18... | collective-permute-start | bytes 1966088
  1234.5 26.9 %collective-permute-start.17 = (bf16[30,10240]{1,0:T(8,128)(2,1)S(1)}, bf16[30,10240]{1,0:T(8,128)(2,1)S(1)}, u32[]{:S(2)}, u32[]{:S(2)}) collective-permute-start(bf16[30,10240]{1,0:T(8,128)(2,1)S(1)} %slice.312), channel_id=1, source_target_pairs={{0,4},{2,6},{4,8},{6,10},{8,12},{10,14},{12,16},{14,18},{16,20},{1... | collective-permute-start | bytes 1843208
  (93 other events, 6484.2 us)
Sparse Core Ops, SparseCore 0:
  11.2 458.8 all-gather.2
  1272.2 24.8 all-reduce.4
where the time goes:
time: 1320 us; the launch traced here: 1310 us
  waiting for transfers between devices  500 us (38%)
  blocking collectives  446 us (34%)
  matrix products  201 us (15%)
  local copies, waits for them, and re-layouts  81.7 us (6%)
  starting transfers between devices  39.8 us (3%)
  other arithmetic  26.8 us (2%)
  between operations  17.1 us (1%)
    all_gather x1, waiting for transfers between devices, side_by_side(): filled = lax.all_gather(both, axis, axis=dim, tiled=True)  451 us
    unnamed x1, blocking collectives  446 us
    dot_general x12, matrix products, reduce_grads(): lax.dot_general(left_side, right_side, (((0,), (0,)), ((), ())), preferre...  78.4 us
    unnamed x209, local copies, waits for them, and re-layouts  38.7 us
    ppermute x16, starting transfers between devices, from_behind(): return lax.ppermute(block, axis, route)  36.1 us
    dot_general x6, matrix products, gained_product(): lax.dot_general(left_side, weight_piece, (((1,), (1,)), ((), ())), prefer...  35 us
    dot_general x6, matrix products, held_scaled(): jnp.dot(scaled, weight_full, preferred_element_type=jnp.float32)  31.1 us
    concatenate x1, local copies, waits for them, and re-layouts, reduce_grads(): jnp.concatenate(blocks, axis=1).astype(jnp.bfloat16)  28.5 us
  transfers between devices with their start and end apart: 20, of which 11 were waited for; matrix products, arithmetic and copies ran while one was open for 6% of the time, Pallas kernels for 0%

commit v1 on v0

v1 whole, which is shorter than its diff:
```python
import functools

import jax
import jax.numpy as jnp
import numpy as np
from jax import lax
from jax.experimental import pallas as pl
from jax.experimental.pallas import tpu as pltpu
from jax.sharding import PartitionSpec as P

D = 960
HEADS = 15
KV_HEADS = 5
HEAD = 64
FF = 2560
SEQ = 128
EPS = 1e-05
BASE = 100000.0

DP = 1024
HALF = DP // 2
QKV = 1600
QKVP = 1664
QK = 1280
ROWS = 30
BF = jnp.bfloat16
F32 = jnp.float32
MESH = pl.DeviceIdType.MESH

CHUNKS = ((0, 0, QKVP), (1, 0, DP), (2, 0, FF), (2, FF, FF), (3, 0, FF))
WIDTHS = (QKVP, DP, 2 * FF, FF)
BACK_ORDER = (4, 2, 3, 1, 0)
N_AG = 18
N_RS = 12


def permutation():
    table = np.zeros((D, DP), np.float32)
    for d in range(D):
        f, r = divmod(d, ROWS)
        y, z, x = f // 8, (f // 2) % 4, f % 2
        h, rr = divmod(r, 16)
        at = (z * 2 + x) * 4 + y if h == 0 else (y * 2 + x) * 4 + z
        table[d, h * HALF + at * 16 + rr] = 1.0
    return table


def lane_frequencies():
    i = np.arange(128) % 32
    return np.power(np.float32(BASE), -(i.astype(np.float32)) * np.float32(2.0 / HEAD))[None, :].astype(np.float32)


def nn(a, b):
    return lax.dot_general(a, b, (((1,), (0,)), ((), ())), preferred_element_type=F32)


def nt(a, b):
    return lax.dot_general(a, b, (((1,), (1,)), ((), ())), preferred_element_type=F32)


def tn(a, b):
    return lax.dot_general(a, b, (((0,), (0,)), ((), ())), preferred_element_type=F32)


def over(total, tile, body):
    whole = total // tile

    @pl.loop(0, whole)
    def _(i):
        body(pl.ds(pl.multiple_of(i * tile, tile), tile))

    if total % tile:
        body(pl.ds(whole * tile, total % tile))


def kernel(
    tok, seg, ga, wq_in, wo_in, gf, wg_in, wd_in, dout, perm, freq,
    acts, igrad, gga, gq, go, ggf, gg, gd,
    wq, wo, wg, wd, *rest,
):
    n = len(CHUNKS)
    (pq, po, pg, pd), rest = rest[:4], rest[4:]
    rb, ra, rx, r3, fin = (rest[k * n:(k + 1) * n] for k in range(5))
    rest = rest[5 * n:]
    (
        raw, draw, xin, din, act, ig, a960, i960,
        qkv, qk, vv, pf, o, h, xn1, xn2, gate, up, mm,
        dgu, dh, da, do, dqkf, dqkv, lt, cosr, sinr, gains,
        ag_s, ag_r, rs_s, rs_r, mi_s, mi_r,
    ) = rest
    weights = (wq, wo, wg, wd)

    sec = lax.axis_index("section")
    f = lax.axis_index("fsdp")
    c = lax.axis_index("ctx")
    y = f // 8
    z = lax.rem(f // 2, 4)
    x = lax.rem(f, 2)
    a = y + c * (z - y)
    cc = z + c * (y - z)

    def at(a_, x_, cc_):
        yy = a_ + c * (cc_ - a_)
        zz = cc_ + c * (a_ - cc_)
        return (sec, (yy * 4 + zz) * 2 + x_, c)

    def mod4(v):
        return lax.rem(v + 4, 4)

    def row(cc_, x_, a_, half=None):
        half = c if half is None else half
        return pl.multiple_of(half * HALF + ((cc_ * 2 + x_) * 4 + a_) * 16, 16)

    sibling = (sec, f, 1 - c)
    partner = (1 - sec, f, c)
    other_x = 1 - x

    def remote(src, dst, ssem, rsem, dev):
        return pltpu.make_async_remote_copy(
            src_ref=src, dst_ref=dst, send_sem=ssem, recv_sem=rsem, device_id=dev, device_id_type=MESH
        )

    barrier = pltpu.get_barrier_semaphore()
    friends = [at(mod4(a + 1), x, cc), at(mod4(a + 2), x, cc), at(mod4(a + 3), x, cc), at(a, other_x, cc),
               at(a, x, mod4(cc + 1)), at(a, x, mod4(cc + 3)), sibling, partner]
    for dev in friends:
        pl.semaphore_signal(barrier, inc=1, device_id=dev, device_id_type=MESH)
    pl.semaphore_wait(barrier, len(friends))

    pending = []

    def send(src, dst, sems, k, dev):
        copy = remote(src, dst, sems[0].at[k], sems[1].at[k], dev)
        copy.start()
        pending.append(copy)

    def arrived(dst, sems, k):
        remote(dst, dst, sems[0].at[k], sems[1].at[k], sibling).wait_recv()

    def drain():
        for copy in pending:
            copy.wait_send()
        pending.clear()

    ag = (ag_s, ag_r)
    rs = (rs_s, rs_r)
    mi = (mi_s, mi_r)

    own_half = pl.ds(pl.multiple_of(64 * c, 64), 64)
    sib_half = pl.ds(pl.multiple_of(64 * (1 - c), 64), 64)
    send(tok.at[1 - c], raw.at[own_half], mi, 0, sibling)
    send(dout.at[1 - c], draw.at[own_half], mi, 1, sibling)
    raw[own_half, :] = tok[c]
    draw[own_half, :] = dout[c]

    gains[...] = jnp.zeros_like(gains)
    gains[0:1, 0:ROWS] = ga[...].astype(F32)
    gains[1:2, 0:ROWS] = gf[...].astype(F32)
    gain_cols = gains[0:8, 0:128].T
    for pack, source, cols in ((pq, wq_in, QKV), (po, wo_in, D), (pg, wg_in, 2 * FF), (pd, wd_in, FF)):
        pack[...] = jnp.zeros_like(pack)
        pack[0:ROWS, 0:cols] = source[...]
    pq[:, QKV:QKV + 2] = gain_cols[0:32, 0:2].astype(BF)
    own16 = pl.ds(pl.multiple_of(16 * c, 16), 16)
    for pack, w in ((pq, wq), (po, wo), (pg, wg), (pd, wd)):
        w[pl.ds(row(cc, x, a), 16), :] = pack[own16, :]

    def ag_piece(m, start, rows):
        w, first, cols = CHUNKS[m]
        return weights[w].at[pl.ds(start, rows), pl.ds(first, cols)]

    def ag_send(m, start, rows, k, dev):
        piece = ag_piece(m, start, rows)
        send(piece, piece, ag, m * N_AG + k, dev)

    def ag_arrived(m, start, rows, k):
        arrived(ag_piece(m, start, rows), ag, m * N_AG + k)

    last_up, last_down = at(a, x, mod4(cc + 1)), at(a, x, mod4(cc + 3))

    def ag0(m):
        for k, step in enumerate((1, 3, 2)):
            ag_send(m, row(cc, x, a), 16, k, at(mod4(a + step), x, cc))

    def ag1(m):
        for k, step in enumerate((1, 3, 2)):
            ag_arrived(m, row(cc, x, mod4(a - step)), 16, k)
        mine = row(cc, x, 0)
        ag_send(m, mine, 64, 3, at(a, other_x, cc))
        ag_send(m, mine, 64, 4, last_up)
        ag_send(m, mine, 64, 5, last_down)
        ag_send(m, mine, 64, 10, sibling)

    def ag2(m):
        theirs = row(cc, other_x, 0)
        ag_arrived(m, theirs, 64, 3)
        ag_send(m, theirs, 64, 6, last_up)
        ag_send(m, theirs, 64, 7, last_down)
        ag_send(m, theirs, 64, 11, sibling)
        below, above = row(mod4(cc - 1), x, 0), row(mod4(cc + 1), x, 0)
        ag_arrived(m, below, 64, 4)
        ag_send(m, below, 64, 8, last_up)
        ag_send(m, below, 64, 12, sibling)
        ag_arrived(m, above, 64, 5)
        ag_send(m, above, 64, 13, sibling)

    def ag3(m):
        below, above = row(mod4(cc - 1), other_x, 0), row(mod4(cc + 1), other_x, 0)
        ag_arrived(m, above, 64, 7)
        ag_send(m, above, 64, 9, last_down)
        ag_send(m, above, 64, 15, sibling)
        ag_arrived(m, below, 64, 6)
        ag_send(m, below, 64, 14, sibling)

    def ag4(m):
        far = row(mod4(cc + 2), x, 0)
        ag_arrived(m, far, 64, 8)
        ag_send(m, far, 64, 16, sibling)
        far = row(mod4(cc + 2), other_x, 0)
        ag_arrived(m, far, 64, 9)
        ag_send(m, far, 64, 17, sibling)

    def ag5(m):
        for k, (step, x_) in enumerate(((0, x), (0, other_x), (3, x), (1, x), (3, other_x), (1, other_x), (2, x), (2, other_x))):
            ag_arrived(m, row(mod4(a + step), x_, 0, 1 - c), 64, 10 + k)

    for m in range(n):
        ag0(m)
    stages = (ag1, ag2, ag3, ag4, ag5)
    for t in range(n + len(stages) - 1):
        for k in reversed(range(len(stages))):
            if 0 <= t - k < n:
                stages[k](t - k)

    places = lax.broadcasted_iota(jnp.int32, (SEQ, SEQ), 0)
    lanes = lax.broadcasted_iota(jnp.int32, (SEQ, SEQ), 1)
    key_seg = jnp.broadcast_to(seg[pl.ds(c, 1), :].astype(F32), (SEQ, SEQ))
    query_seg = key_seg.T
    allowed = (key_seg == query_seg) & (lanes <= places)
    earlier = jnp.sum(jnp.where(key_seg < query_seg, 1.0, 0.0), axis=1, keepdims=True)
    pos = places.astype(F32) - earlier
    angle = pos * freq[...]
    first_half = lax.rem(lanes, HEAD) < HEAD // 2
    cosr[...] = jnp.cos(angle)
    sinr[...] = jnp.where(first_half, -jnp.sin(angle), jnp.sin(angle))

    def swap(u):
        return jnp.where(first_half, pltpu.roll(u, 96, 1), pltpu.roll(u, 32, 1))

    arrived(raw.at[sib_half], mi, 0)
    arrived(draw.at[sib_half], mi, 1)
    drain()

    @pl.when(sec == 0)
    def _():
        xin[...] = nn(raw[...], perm[...]).astype(BF)

    @pl.when(sec == 1)
    def _():
        din[...] = nn(draw[...], perm[...]).astype(BF)
        arrived(xin, mi, 2)

    gain_rows = wq[:, 1536:1664].astype(F32).T[64:72, :]
    gain_one = gain_rows[0:1, :]
    gain_two = gain_rows[1:2, :]

    def norm(v):
        inverse = lax.rsqrt(jnp.sum(v * v, axis=1, keepdims=True) * (1.0 / D) + EPS)
        return v * inverse, inverse

    def norm_back(d, normal, inverse):
        return inverse * (d - normal * (jnp.sum(normal * d, axis=1, keepdims=True) * (1.0 / D)))

    xv = xin[...].astype(F32)
    xhat, _ = norm(xv)
    xn1[...] = (xhat * gain_one).astype(BF)

    def body_qkv(cols):
        qkv[:, cols] = nn(xn1[...], wq[:, cols])

    over(QKVP, 512, body_qkv)
    for t in range(QK // 128):
        cols = pl.ds(128 * t, 128)
        u = qkv[:, cols]
        qk[:, cols] = (u * cosr[...] + swap(u) * sinr[...]).astype(BF)
    vv[...] = qkv[:, QK:QKVP].astype(BF)
    o[:, HEADS * HEAD:] = jnp.zeros((SEQ, DP - HEADS * HEAD), BF)
    for g in range(KV_HEADS):
        k_g = qk[:, D + HEAD * g:D + HEAD * (g + 1)]
        v_g = vv[:, HEAD * g:HEAD * (g + 1)]
        for j in range(HEADS // KV_HEADS):
            hd = g * 3 + j
            s = nt(qk[:, HEAD * hd:HEAD * (hd + 1)], k_g) * (HEAD ** -0.5)
            s = jnp.where(allowed, s, -1e30)
            e = jnp.exp(s - jnp.max(s, axis=1, keepdims=True))
            p = e / jnp.sum(e, axis=1, keepdims=True)
            pf[hd] = p
            o[:, HEAD * hd:HEAD * (hd + 1)] = nn(p.astype(BF), v_g).astype(BF)

    def body_out(rows):
        h[:, rows] = xin[:, rows].astype(F32) + nt(o[...], wo[rows, :])

    over(DP, 256, body_out)
    xhat, _ = norm(h[...])
    xn2[...] = (xhat * gain_two).astype(BF)

    def body_gu(cols):
        first = cols.start
        g_ = nn(xn2[...], wg[:, pl.ds(first, 512)])
        u_ = nn(xn2[...], wg[:, pl.ds(pl.multiple_of(first + FF, 512), 512)])
        gate[:, cols] = g_
        up[:, cols] = u_
        mm[:, cols] = (g_ * jax.nn.sigmoid(g_) * u_).astype(BF)

    over(FF, 512, body_gu)

    def body_down(rows):
        act[:, rows] = (h[:, rows] + nt(mm[...], wd[rows, :])).astype(BF)

    over(DP, 256, body_down)

    @pl.when(sec == 0)
    def _():
        remote(act, xin, mi_s.at[2], mi_r.at[2], partner).start()

    a960[...] = nt(act[...], perm[...]).astype(BF)
    acts[c] = a960[own_half, :]
    send(a960.at[sib_half], acts.at[c], mi, 4, sibling)

    @pl.when(sec == 0)
    def _():
        remote(act, xin, mi_s.at[2], mi_r.at[2], partner).wait_send()
        arrived(din, mi, 3)

    def body_dm(cols):
        dm = nn(din[...], wd[:, cols])
        g_ = gate[:, cols]
        u_ = up[:, cols]
        sg = jax.nn.sigmoid(g_)
        dgu[:, cols] = (dm * u_ * sg * (1.0 + g_ * (1.0 - sg))).astype(BF)
        dgu[:, pl.ds(pl.multiple_of(cols.start + FF, 512), 512)] = (dm * g_ * sg).astype(BF)

    over(FF, 512, body_dm)

    def body_dxn2(rows):
        dh[:, rows] = nt(dgu[...], wg[rows, :])

    over(DP, 256, body_dxn2)
    xhat, inv = norm(h[...])
    dhv = din[...].astype(F32) + norm_back(dh[...] * gain_two, xhat, inv)
    dh[...] = dhv
    da[...] = dhv.astype(BF)

    def body_do(cols):
        do[:, cols] = nn(da[...], wo[:, cols]).astype(BF)

    over(DP, 512, body_do)
    scale = HEAD ** -0.5
    dqkv[:, QKV:] = jnp.zeros((SEQ, QKVP - QKV), BF)
    for g in range(KV_HEADS):
        k_g = qk[:, D + HEAD * g:D + HEAD * (g + 1)]
        v_g = vv[:, HEAD * g:HEAD * (g + 1)]
        dk, dv = None, None
        for j in range(HEADS // KV_HEADS):
            hd = g * 3 + j
            hc = slice(HEAD * hd, HEAD * (hd + 1))
            p = pf[hd]
            do_h = do[:, hc]
            dp = nt(do_h, v_g)
            ds = (p * (dp - jnp.sum(dp * p, axis=1, keepdims=True))).astype(BF)
            dqkf[:, hc] = nn(ds, k_g) * scale
            dk_h = tn(ds, qk[:, hc])
            dv_h = tn(p.astype(BF), do_h)
            dk = dk_h if dk is None else dk + dk_h
            dv = dv_h if dv is None else dv + dv_h
        dqkf[:, D + HEAD * g:D + HEAD * (g + 1)] = dk * scale
        dqkv[:, QK + HEAD * g:QK + HEAD * (g + 1)] = dv.astype(BF)
    for t in range(QK // 128):
        cols = pl.ds(128 * t, 128)
        u = dqkf[:, cols]
        dqkv[:, cols] = (u * cosr[...] - swap(u) * sinr[...]).astype(BF)

    def body_dxn1(rows):
        h[:, rows] = nt(dqkv[...], wq[rows, :])

    over(DP, 256, body_dxn1)
    xhat, inv = norm(xin[...].astype(F32))
    ig[...] = (dh[...] + norm_back(h[...] * gain_one, xhat, inv)).astype(BF)

    @pl.when(sec == 1)
    def _():
        remote(ig, din, mi_s.at[3], mi_r.at[3], partner).start()

    def wgrad(left, right, w, first, cols):
        lt[...] = left[...].T

        def body(tile):
            width = tile.size
            mine = pl.ds(pl.multiple_of(tile.start + first, 128), width)
            for r in range(4):
                rows = pl.ds(256 * r, 256)
                w[rows, mine] = nn(lt[rows, :], right[:, mine]).astype(BF)

        over(cols, 512, body)

    pairs = ((xn1, dqkv), (da, o), (xn2, dgu), (din, mm))

    def rs_piece(m, start, rows):
        w, first, cols = CHUNKS[m]
        return weights[w].at[pl.ds(start, rows), pl.ds(first, cols)]

    def add_in(m, start, rows, source, source_row):
        w, first, cols = CHUNKS[m]
        ref = weights[w]

        def body(tile):
            mine = pl.ds(pl.multiple_of(tile.start + first, 128), tile.size)
            ref[pl.ds(start, rows), mine] = ref[pl.ds(start, rows), mine] + source[pl.ds(source_row, rows), tile]

        over(cols, 512, body)

    def rs_send(m, start, rows, dst, k, dev):
        send(rs_piece(m, start, rows), dst, rs, m * N_RS + k, dev)

    def rs_arrived(m, dst, k):
        arrived(dst, rs, m * N_RS + k)

    def part(m, k):
        return ra[m].at[pl.ds(64 * k, 64)]

    nxt, prv, far = mod4(cc + 1), mod4(cc - 1), mod4(cc + 2)

    def rs0(m):
        w, first, cols = CHUNKS[m]
        wgrad(*pairs[w], weights[w], first, cols)
        rs_send(m, pl.multiple_of((1 - c) * HALF, HALF), HALF, rb[m], 0, sibling)

    def rs1(m):
        rs_arrived(m, rb[m], 0)
        add_in(m, pl.multiple_of(c * HALF, HALF), HALF, rb[m], 0)
        rs_send(m, row(far, 0, 0), 64, part(m, 0), 1, last_up)
        rs_send(m, row(far, 1, 0), 64, part(m, 1), 2, last_down)
        rs_send(m, row(nxt, 1, 0), 64, part(m, 2), 3, last_up)
        rs_send(m, row(prv, 0, 0), 64, part(m, 3), 4, last_down)

    def rs2(m):
        rs_arrived(m, part(m, 0), 1)
        add_in(m, row(nxt, 0, 0), 64, ra[m], 0)
        rs_send(m, row(nxt, 0, 0), 64, part(m, 4), 5, last_up)
        rs_arrived(m, part(m, 1), 2)
        add_in(m, row(prv, 1, 0), 64, ra[m], 64)
        rs_send(m, row(prv, 1, 0), 64, part(m, 5), 6, last_down)

    def rs3(m):
        for k, x_, sem in ((2, 1, 3), (3, 0, 4), (4, 0, 5), (5, 1, 6)):
            rs_arrived(m, part(m, k), sem)
            add_in(m, row(cc, x_, 0), 64, ra[m], 64 * k)
        rs_send(m, row(cc, other_x, 0), 64, rx[m], 7, at(a, other_x, cc))

    def rs4(m):
        rs_arrived(m, rx[m], 7)
        add_in(m, row(cc, x, 0), 64, rx[m], 0)
        for k, step in enumerate((1, 3, 2)):
            to = mod4(a + step)
            rs_send(m, row(cc, x, to), 16, r3[m].at[pl.ds(16 * k, 16)], 8 + k, at(to, x, cc))

    def rs5(m):
        w, first, cols = CHUNKS[m]
        for k in range(3):
            rs_arrived(m, r3[m].at[pl.ds(16 * k, 16)], 8 + k)
        total = weights[w][pl.ds(row(cc, x, a), 16), pl.ds(first, cols)].astype(F32)
        for k in range(3):
            total = total + r3[m][pl.ds(16 * k, 16), :].astype(F32)
        fin[m][own16, :] = total
        mine = fin[m].at[own16]
        send(mine, mine, rs, m * N_RS + 11, sibling)

    def rs6(m):
        rs_arrived(m, fin[m].at[pl.ds(pl.multiple_of(16 * (1 - c), 16), 16)], 11)

    stages = (rs0, rs1, rs2, rs3, rs4, rs5, rs6)
    for t in range(n + len(stages) - 1):
        for k in reversed(range(len(stages))):
            if 0 <= t - k < n:
                stages[k](BACK_ORDER[t - k])

    gq[...] = fin[0][0:ROWS, 0:QKV]
    go[...] = fin[1][0:ROWS, 0:D]
    gg[:, 0:FF] = fin[2][0:ROWS, :]
    gg[:, FF:] = fin[3][0:ROWS, :]
    gd[...] = fin[4][0:ROWS, :]
    sum_one = jnp.sum(fin[0][:, 0:QKV] * pq[:, 0:QKV].astype(F32), axis=1, keepdims=True)
    sum_two = jnp.sum(
        fin[2][...] * pg[:, 0:FF].astype(F32) + fin[3][...] * pg[:, FF:].astype(F32), axis=1, keepdims=True
    )
    gga[...] = jnp.broadcast_to(sum_one, (32, 128)).T[0:1, 0:ROWS] / ga[...].astype(F32)
    ggf[...] = jnp.broadcast_to(sum_two, (32, 128)).T[0:1, 0:ROWS] / gf[...].astype(F32)

    i960[...] = nt(ig[...], perm[...]).astype(BF)
    igrad[c] = i960[own_half, :]
    send(i960.at[sib_half], igrad.at[c], mi, 5, sibling)
    arrived(acts.at[1 - c], mi, 4)
    arrived(igrad.at[1 - c], mi, 5)

    @pl.when(sec == 1)
    def _():
        remote(ig, din, mi_s.at[3], mi_r.at[3], partner).wait_send()

    drain()


def per_device(tokens, segments, gain_attn, w_qkv, w_out, gain_ffn, w_gu, w_down, d_out):
    n = len(CHUNKS)
    vmem = pl.BlockSpec(memory_space=pltpu.VMEM)
    per_chunk = lambda rows, kind: [pltpu.VMEM((rows, cols), kind) for _, _, cols in CHUNKS]
    scratch = (
        [pltpu.VMEM((DP, w), BF) for w in WIDTHS]
        + [pltpu.VMEM((32, w), BF) for w in WIDTHS]
        + per_chunk(HALF, BF) + per_chunk(384, BF) + per_chunk(64, BF) + per_chunk(48, BF) + per_chunk(32, F32)
        + [
            pltpu.VMEM((SEQ, D), BF), pltpu.VMEM((SEQ, D), BF),
            pltpu.VMEM((SEQ, DP), BF), pltpu.VMEM((SEQ, DP), BF),
            pltpu.VMEM((SEQ, DP), BF), pltpu.VMEM((SEQ, DP), BF),
            pltpu.VMEM((SEQ, D), BF), pltpu.VMEM((SEQ, D), BF),
            pltpu.VMEM((SEQ, QKVP), F32), pltpu.VMEM((SEQ, QK), BF), pltpu.VMEM((SEQ, QKVP - QK), BF),
            pltpu.VMEM((HEADS, SEQ, SEQ), F32), pltpu.VMEM((SEQ, DP), BF), pltpu.VMEM((SEQ, DP), F32),
            pltpu.VMEM((SEQ, DP), BF), pltpu.VMEM((SEQ, DP), BF),
            pltpu.VMEM((SEQ, FF), F32), pltpu.VMEM((SEQ, FF), F32), pltpu.VMEM((SEQ, FF), BF),
            pltpu.VMEM((SEQ, 2 * FF), BF), pltpu.VMEM((SEQ, DP), F32),
            pltpu.VMEM((SEQ, DP), BF), pltpu.VMEM((SEQ, DP), BF),
            pltpu.VMEM((SEQ, QK), F32), pltpu.VMEM((SEQ, QKVP), BF), pltpu.VMEM((DP, SEQ), BF),
            pltpu.VMEM((SEQ, SEQ), F32), pltpu.VMEM((SEQ, SEQ), F32), pltpu.VMEM((8, 128), F32),
        ]
        + [pltpu.SemaphoreType.DMA((n * N_AG,))] * 2
        + [pltpu.SemaphoreType.DMA((n * N_RS,))] * 2
        + [pltpu.SemaphoreType.DMA((6,))] * 2
    )
    shape = jax.ShapeDtypeStruct
    out = pl.pallas_call(
        kernel,
        out_shape=(
            shape(tokens.shape, BF), shape(tokens.shape, BF),
            shape((1, ROWS), F32), shape((ROWS, QKV), F32), shape((ROWS, D), F32),
            shape((1, ROWS), F32), shape((ROWS, 2 * FF), F32), shape((ROWS, FF), F32),
        ),
        in_specs=[vmem] * 11,
        out_specs=(vmem,) * 8,
        scratch_shapes=scratch,
        compiler_params=pltpu.CompilerParams(
            collective_id=0, has_side_effects=True, vmem_limit_bytes=63 * 1024 * 1024
        ),
    )(
        tokens, segments, gain_attn, w_qkv[0], w_out[0], gain_ffn, w_gu[0], w_down[0], d_out,
        jnp.asarray(permutation(), BF), jnp.asarray(lane_frequencies(), F32),
    )
    acts, igrad, gga, gq, go, ggf, gg, gd = out
    return acts[None], igrad[None], gga, gq[None], go[None], ggf, gg[None], gd[None]


def solution(mesh):
    in_specs = (
        P(None, ("fsdp", "ctx"), None),
        P(None, "fsdp"),
        P("section", "fsdp"),
        P("section", "fsdp", None),
        P("section", "fsdp", None),
        P("section", "fsdp"),
        P("section", "fsdp", None),
        P("section", "fsdp", None),
        P(None, ("fsdp", "ctx"), None),
    )
    out_specs = (
        P("section", None, ("fsdp", "ctx"), None),
        P("section", None, ("fsdp", "ctx"), None),
        P("section", "fsdp"),
        P("section", "fsdp", None),
        P("section", "fsdp", None),
        P("section", "fsdp"),
        P("section", "fsdp", None),
        P("section", "fsdp", None),
    )
    return jax.shard_map(
        per_device, mesh=mesh, in_specs=in_specs, out_specs=out_specs, check_vma=False
    )
```

time: 1320 us -> 229 us (0.17)
  waiting for transfers between devices: 500 us -> 0 us
  blocking collectives: 446 us -> 0 us
  Pallas kernels: 0 us -> 218 us
  matrix products: 201 us -> 0 us
  local copies, waits for them, and re-layouts: 81.7 us -> 10.5 us
  starting transfers between devices: 39.8 us -> 0 us
  other arithmetic: 26.8 us -> 0 us
  between operations: 17.1 us -> 0.68 us
    all_gather x1 -> x0, waiting for transfers between devices: 451 us -> none  [side_by_side(): filled = lax.all_gather(both, axis, axis=dim, tiled=True)]
    unnamed x1 -> x0, blocking collectives: 446 us -> none
    pallas_call x0 -> x1, Pallas kernels: none -> 218 us  [per_device(): pl.pallas_call(kernel, out_shape=(shape(tokens.shape, BF), shape(tokens.s...]
    dot_general x54 -> x0, matrix products: 201 us -> none  [the longest x12 78.4 us: reduce_grads(): lax.dot_general(left_side, right_side, (((0,), (0,)), ((), ())), preferre...]
    ppermute x16 -> x0, starting transfers between devices: 36.1 us -> none  [from_behind(): return lax.ppermute(block, axis, route)]
    concatenate x6 -> x0, local copies, waits for them, and re-layouts: 32 us -> none  [the longest x1 28.5 us: reduce_grads(): jnp.concatenate(blocks, axis=1).astype(jnp.bfloat16)]
    unnamed x209 -> x16, local copies, waits for them, and re-layouts: 38.7 us -> 10.5 us
    unnamed x4 -> x0, waiting for transfers between devices: 20.2 us -> none
  transfers between devices with their start and end apart: 20 -> 0, of which waited for: 11 -> 0; matrix products, arithmetic and copies ran while one was open for 6% -> 0% of each run, Pallas kernels for 0% -> 0%
where the time goes in v1:
time: 229 us
  Pallas kernels  218 us (95%)
  local copies, waits for them, and re-layouts  10.5 us (5%)
    pallas_call x1, Pallas kernels, per_device(): pl.pallas_call(kernel, out_shape=(shape(tokens.shape, BF), shape(tokens.s...  218 us
    unnamed x16, local copies, waits for them, and re-layouts  10.5 us

profile of v1, /device:TPU:1, one launch (start us, length us, event | category | flops | bytes accessed | tf_op | source)
XLA Modules:
  0.0 228.9 jit_solution(1310125478981346980)
XLA Ops:
  0.6 217.7 %shard_map.170 = (bf16[2,64,960]{2,1,0:T(8,128)(2,1)}, bf16[2,64,960]{2,1,0:T(8,128)(2,1)}, f32[1,30]{1,0:T(1,128)}, f32[30,1600]{1,0:T(8,128)}, f32[30,960]{1,0...) custom-call(bf16[2,64,960]{2,1,0:T(8,128)(2,1)} %tok.1, s32[2,128]{1,0:T(2,128)} %seg.1, ...), custom_call_target="tpu_custom_call" | custom-call | tf_op jit(solution)/shard_map/pallas_call | solution.py:539
  218.4 0.0 copy-start.1
  218.4 0.0 copy-start
  218.4 0.0 copy-start.3
  218.4 0.0 copy-start.2
  218.4 1.7 copy.20
  220.1 1.8 copy.19
  222.0 2.0 copy.22
  224.0 2.5 %copy.21 = f32[1,30,5120]{2,0,1:T(1,128)} copy(f32[1,30,5120]{2,1,0:T(8,128)} %bitcast.10) | data formatting | bytes 1228800
  226.5 0.0 copy-done.1
  226.5 0.7 copy.27
  227.2 0.0 copy-done
  227.2 0.7 copy.28
  227.9 0.0 copy-done.3
  227.9 0.5 copy.29
  228.4 0.0 copy-done.2
  228.4 0.5 copy.30
Async XLA Ops:
  218.4 8.1 %copy-start.1 = (bf16[2,64,960]{2,1,0:T(8,128)(2,1)S(1)}, bf16[2,64,960]{2,1,0:T(8,128)(2,1)}, u32[]{:S(2)}) copy-start(bf16[2,64,960]{2,1,0:T(8,128)(2,1)} %get-tuple-element.16) | copy-start | bytes 737284
  218.4 8.8 %copy-start = (bf16[2,64,960]{2,1,0:T(8,128)(2,1)S(1)}, bf16[2,64,960]{2,1,0:T(8,128)(2,1)}, u32[]{:S(2)}) copy-start(bf16[2,64,960]{2,1,0:T(8,128)(2,1)} %get-tuple-element.17) | copy-start | bytes 737284
  218.4 9.5 %copy-start.3 = (f32[1,30]{1,0:T(1,128)S(1)}, f32[1,30]{1,0:T(1,128)}, u32[]{:S(2)}) copy-start(f32[1,30]{1,0:T(1,128)} %get-tuple-element.42) | copy-start | bytes 364
  218.4 10.0 %copy-start.2 = (f32[1,30]{1,0:T(1,128)S(1)}, f32[1,30]{1,0:T(1,128)}, u32[]{:S(2)}) copy-start(f32[1,30]{1,0:T(1,128)} %get-tuple-element.45) | copy-start | bytes 364

commit v2 on v1

v2 whole, which is shorter than its diff:
```python
import functools

import jax
import jax.numpy as jnp
import numpy as np
from jax import lax
from jax.experimental import pallas as pl
from jax.experimental.pallas import tpu as pltpu
from jax.sharding import PartitionSpec as P

D = 960
HEADS = 15
KV_HEADS = 5
HEAD = 64
FF = 2560
SEQ = 128
EPS = 1e-05
BASE = 100000.0

DP = 1024
HALF = DP // 2
QKV = 1600
QKVP = 1664
QK = 1280
ROWS = 30
BF = jnp.bfloat16
F32 = jnp.float32
MESH = pl.DeviceIdType.MESH

PART = FF // 2
CHUNKS = (
    (0, 0, QKVP), (1, 0, DP), (2, 0, PART), (2, FF, PART), (2, PART, PART), (2, FF + PART, PART), (3, 0, PART), (3, PART, PART),
)
WIDTHS = (QKVP, DP, 2 * FF, FF)
BACK_ORDER = (6, 7, 2, 3, 4, 5, 1, 0)
N_AG = 18
N_RS = 12


def permutation():
    table = np.zeros((D, DP), np.float32)
    for d in range(D):
        f, r = divmod(d, ROWS)
        y, z, x = f // 8, (f // 2) % 4, f % 2
        h, rr = divmod(r, 16)
        at = (z * 2 + x) * 4 + y if h == 0 else (y * 2 + x) * 4 + z
        table[d, h * HALF + at * 16 + rr] = 1.0
    return table


def lane_frequencies():
    i = np.arange(128) % 32
    return np.power(np.float32(BASE), -(i.astype(np.float32)) * np.float32(2.0 / HEAD))[None, :].astype(np.float32)


def nn(a, b):
    return lax.dot_general(a, b, (((1,), (0,)), ((), ())), preferred_element_type=F32)


def nt(a, b):
    return lax.dot_general(a, b, (((1,), (1,)), ((), ())), preferred_element_type=F32)


def tn(a, b):
    return lax.dot_general(a, b, (((0,), (0,)), ((), ())), preferred_element_type=F32)


def over(total, tile, body):
    whole = total // tile

    @pl.loop(0, whole)
    def _(i):
        body(pl.ds(pl.multiple_of(i * tile, tile), tile))

    if total % tile:
        body(pl.ds(whole * tile, total % tile))


def kernel(
    tok, seg, ga, wq_in, wo_in, gf, wg_in, wd_in, dout, perm_in, freq,
    acts, igrad, gga, ggf, *rest,
):
    n = len(CHUNKS)
    fin, rest = rest[:n], rest[n:]
    (wq, wo, wg, wd), rest = rest[:4], rest[4:]
    shards, rest = rest[:4], rest[4:]
    (pq, po, pg, pd), rest = rest[:4], rest[4:]
    rb, ra, rx, r3 = (rest[k * n:(k + 1) * n] for k in range(4))
    rest = rest[4 * n:]
    lts, rest = rest[:4], rest[4:]
    (
        perm, raw, draw, xin, din, act, ig, a960, i960,
        qkv, qk, vv, pf, o, h, xn1, xn2, gate, up, mm,
        dgu, dh, da, do, dps, dsb, dqkf, dqkv, cosr, sinr, gains,
        in_s, ag_s, ag_r, rs_s, rs_r, mi_s, mi_r,
    ) = rest
    weights = (wq, wo, wg, wd)

    sec = lax.axis_index("section")
    f = lax.axis_index("fsdp")
    c = lax.axis_index("ctx")
    y = f // 8
    z = lax.rem(f // 2, 4)
    x = lax.rem(f, 2)
    a = y + c * (z - y)
    cc = z + c * (y - z)
    other_x = 1 - x

    def at(a_, x_, cc_):
        yy = a_ + c * (cc_ - a_)
        zz = cc_ + c * (a_ - cc_)
        return (sec, (yy * 4 + zz) * 2 + x_, c)

    def mod4(v):
        return lax.rem(v + 4, 4)

    def row(cc_, x_, a_, half=None):
        half = c if half is None else half
        return pl.multiple_of(half * HALF + ((cc_ * 2 + x_) * 4 + a_) * 16, 16)

    own_half = pl.ds(pl.multiple_of(64 * c, 64), 64)
    sib_half = pl.ds(pl.multiple_of(64 * (1 - c), 64), 64)
    own16 = pl.ds(pl.multiple_of(16 * c, 16), 16)
    fetch = [
        pltpu.make_async_copy(src, dst, in_s.at[k])
        for k, (src, dst) in enumerate((
            (wq_in, shards[0]), (wo_in, shards[1]), (wg_in, shards[2]), (wd_in, shards[3]),
            (tok.at[c], raw.at[own_half]), (dout.at[c], draw.at[own_half]), (perm_in, perm),
        ))
    ]
    for copy in fetch:
        copy.start()

    sibling = (sec, f, 1 - c)
    partner = (1 - sec, f, c)
    last_up, last_down = at(a, x, mod4(cc + 1)), at(a, x, mod4(cc + 3))
    over_x = at(a, other_x, cc)
    first_to = [at(mod4(a + step), x, cc) for step in (1, 3, 2)]

    barrier = pltpu.get_barrier_semaphore()
    friends = first_to + [over_x, last_up, last_down, sibling, partner]
    for dev in friends:
        pl.semaphore_signal(barrier, inc=1, device_id=dev, device_id_type=MESH)

    gains[...] = jnp.zeros_like(gains)
    gains[0:1, 0:ROWS] = ga[...].astype(F32)
    gains[1:2, 0:ROWS] = gf[...].astype(F32)
    gain_cols = gains[0:8, 0:128].T
    pl.semaphore_wait(barrier, len(friends))

    def remote(src, dst, ssem, rsem, dev):
        return pltpu.make_async_remote_copy(
            src_ref=src, dst_ref=dst, send_sem=ssem, recv_sem=rsem, device_id=dev, device_id_type=MESH
        )

    own_cols = [pl.ds(256 * k, 256) for k in range(4)]
    single = (
        [(tok.at[1 - c], raw.at[own_half], sibling), (dout.at[1 - c], draw.at[own_half], sibling)]
        + [(act.at[:, cols], xin.at[:, cols], partner) for cols in own_cols]
        + [(ig, din, partner), (a960.at[sib_half], acts.at[c], sibling), (i960.at[sib_half], igrad.at[c], sibling)]
    )

    def one(k):
        src, dst, dev = single[k]
        return remote(src, dst, mi_s.at[k], mi_r.at[k], dev)

    steps4 = range(4)
    xs = (x, other_x)
    mine = {(d, s): row(mod4(cc + d), xs[s], 0) for d in steps4 for s in range(2)}
    theirs = {(d, s): row(mod4(a + d), xs[s], 0, 1 - c) for d in steps4 for s in range(2)}
    slab = [row(cc, x, mod4(a + d)) for d in steps4]
    ag_table = [
        (slab[0], slab[3], 16, first_to[0]),
        (slab[0], slab[1], 16, first_to[1]),
        (slab[0], slab[2], 16, first_to[2]),
        (mine[0, 0], mine[0, 1], 64, over_x),
        (mine[0, 0], mine[3, 0], 64, last_up),
        (mine[0, 0], mine[1, 0], 64, last_down),
        (mine[0, 1], mine[3, 1], 64, last_up),
        (mine[0, 1], mine[1, 1], 64, last_down),
        (mine[3, 0], mine[2, 0], 64, last_up),
        (mine[1, 1], mine[2, 1], 64, last_down),
    ] + [
        (mine[key], theirs[key], 64, sibling)
        for key in ((0, 0), (0, 1), (3, 0), (1, 0), (3, 1), (1, 1), (2, 0), (2, 1))
    ]

    def ag_copy(m, k, arriving=False):
        w, first, cols = CHUNKS[m]
        source, landing, rows, dev = ag_table[k]
        piece = weights[w].at[pl.ds(landing if arriving else source, rows), pl.ds(first, cols)]
        return remote(piece, piece, ag_s.at[m * N_AG + k], ag_r.at[m * N_AG + k], dev)

    def ag_send(m, *ks):
        for k in ks:
            ag_copy(m, k).start()

    def ag_wait(m, *ks):
        for k in ks:
            ag_copy(m, k, True).wait_recv()

    def ag1(m):
        ag_wait(m, 0, 1, 2)
        ag_send(m, 4, 5, 3, 10)

    def ag2(m):
        ag_wait(m, 3)
        ag_send(m, 6, 7, 11)
        ag_wait(m, 4)
        ag_send(m, 8, 12)
        ag_wait(m, 5)
        ag_send(m, 13)

    def ag3(m):
        ag_wait(m, 7)
        ag_send(m, 9, 15)
        ag_wait(m, 6)
        ag_send(m, 14)

    def ag4(m):
        ag_wait(m, 8)
        ag_send(m, 16)
        ag_wait(m, 9)
        ag_send(m, 17)

    def ag5(m):
        ag_wait(m, *range(10, 18))

    def ag_step(t):
        for stage, late in ((ag1, 0), (ag5, 4), (ag4, 3), (ag3, 2), (ag2, 1)):
            if 0 <= t - late < n:
                stage(t - late)

    def ag_drain():
        for m in range(n):
            for k in range(N_AG):
                ag_copy(m, k).wait_send()

    one(0).start()
    for w, (pack, cols) in enumerate(((pq, QKV), (po, D), (pg, 2 * FF), (pd, FF))):
        if cols < pack.shape[1]:
            pack[:, cols:] = jnp.zeros((32, pack.shape[1] - cols), BF)
        pack[16:32, :] = jnp.zeros((16, pack.shape[1]), BF)
        fetch[w].wait()
        pack[0:ROWS, 0:cols] = shards[w][...]
        if w == 0:
            pack[:, QKV:QKV + 2] = gain_cols[0:32, 0:2].astype(BF)
        weights[w][pl.ds(slab[0], 16), :] = pack[own16, :]
        for m in range(n):
            if CHUNKS[m][0] == w:
                ag_send(m, 0, 1, 2)
    one(1).start()

    places = lax.broadcasted_iota(jnp.int32, (SEQ, SEQ), 0)
    lanes = lax.broadcasted_iota(jnp.int32, (SEQ, SEQ), 1)
    key_seg = jnp.broadcast_to(seg[pl.ds(c, 1), :].astype(F32), (SEQ, SEQ))
    query_seg = key_seg.T
    allowed = (key_seg == query_seg) & (lanes <= places)
    earlier = jnp.sum(jnp.where(key_seg < query_seg, 1.0, 0.0), axis=1, keepdims=True)
    pos = places.astype(F32) - earlier
    angle = pos * freq[...]
    first_half = lax.rem(lanes, HEAD) < HEAD // 2
    cosr[...] = jnp.cos(angle)
    sinr[...] = jnp.where(first_half, -jnp.sin(angle), jnp.sin(angle))

    def swap(u):
        return jnp.where(first_half, pltpu.roll(u, 96, 1), pltpu.roll(u, 32, 1))

    ag_step(0)
    for copy in fetch[4:]:
        copy.wait()
    for k in range(2):
        src, _, dev = single[k]
        remote(src, (raw, draw)[k].at[sib_half], mi_s.at[k], mi_r.at[k], dev).wait_recv()

    @pl.when(sec == 0)
    def _():
        xin[...] = nn(raw[...], perm[...]).astype(BF)

    @pl.when(sec == 1)
    def _():
        din[...] = nn(draw[...], perm[...]).astype(BF)

    def ag_first(*ts):
        @pl.when(sec == 0)
        def _():
            for t in ts:
                ag_step(t)

    @pl.when(sec == 1)
    def _():
        for t in range(1, n + 4):
            ag_step(t)
        ag_drain()
        for k in range(2, 6):
            one(k).wait_recv()

    ag_first(1, 2, 3, 4)

    def norm(v):
        inverse = lax.rsqrt(jnp.sum(v * v, axis=1, keepdims=True) * (1.0 / D) + EPS)
        return v * inverse, inverse

    def norm_back(d, normal, inverse):
        return inverse * (d - normal * (jnp.sum(normal * d, axis=1, keepdims=True) * (1.0 / D)))

    gains[...] = wq[:, 1536:1664].astype(F32).T[64:72, :]
    xhat, _ = norm(xin[...].astype(F32))
    xn1[...] = (xhat * gains[0:1, :]).astype(BF)
    qkv[...] = nn(xn1[...], wq[...])
    for t in range(QK // 128):
        cols = pl.ds(128 * t, 128)
        u = qkv[:, cols]
        qk[:, cols] = (u * cosr[...] + swap(u) * sinr[...]).astype(BF)
    vv[...] = qkv[:, QK:QKVP].astype(BF)
    ag_first(5)
    group = HEADS // KV_HEADS

    def head(hd):
        return slice(HEAD * hd, HEAD * (hd + 1))

    def key_of(hd):
        return qk[:, head(HEADS + hd // group)]

    def value_of(hd):
        return vv[:, head(hd // group)]

    scale = HEAD ** -0.5
    for hd in range(HEADS):
        pf[hd] = nt(qk[:, head(hd)], key_of(hd))
    for hd in range(HEADS):
        s = jnp.where(allowed, pf[hd] * scale, -1e30)
        e = jnp.exp(s - jnp.max(s, axis=1, keepdims=True))
        pf[hd] = e / jnp.sum(e, axis=1, keepdims=True)
    ag_first(6)
    o[:, HEADS * HEAD:] = jnp.zeros((SEQ, DP - HEADS * HEAD), BF)
    for hd in range(HEADS):
        o[:, head(hd)] = nn(pf[hd].astype(BF), value_of(hd)).astype(BF)
    h[...] = xin[...].astype(F32) + nt(o[...], wo[...])
    xhat, _ = norm(h[...])
    xn2[...] = (xhat * gains[1:2, :]).astype(BF)
    ag_first(7)

    def gated(j):
        cols = pl.ds(PART * j, PART)
        gate[:, cols] = nn(xn2[...], wg[:, cols])
        up[:, cols] = nn(xn2[...], wg[:, pl.ds(FF + PART * j, PART)])
        g_ = gate[:, cols]
        mm[:, cols] = (g_ * jax.nn.sigmoid(g_) * up[:, cols]).astype(BF)

    gated(0)
    ag_first(8, 9)
    gated(1)
    ag_first(10)
    dh[...] = h[...] + nt(mm[:, 0:PART], wd[:, 0:PART])
    ag_first(11)
    for k, cols in enumerate(own_cols):
        act[:, cols] = (dh[:, cols] + nt(mm[:, PART:], wd[cols, PART:])).astype(BF)

        @pl.when(sec == 0)
        def _():
            one(2 + k).start()

    @pl.when(sec == 0)
    def _():
        ag_drain()
        for k in range(2, 6):
            one(k).wait_send()
        one(6).wait_recv()

    pairs = ((xn1, dqkv), (da, o), (xn2, dgu), (din, mm))
    last_at = [mod4(cc + d) for d in steps4]
    block = {(d, x_): row(last_at[d], x_, 0) for d in steps4 for x_ in range(2)}
    lower = pl.multiple_of(c * HALF, HALF)
    upper = pl.multiple_of((1 - c) * HALF, HALF)
    rs_rows = (
        [(upper, HALF, sibling), (block[2, 0], 64, last_up), (block[2, 1], 64, last_down), (block[1, 1], 64, last_up),
         (block[3, 0], 64, last_down), (block[1, 0], 64, last_up), (block[3, 1], 64, last_down), (mine[0, 1], 64, over_x)]
        + [(slab[step], 16, first_to[k]) for k, step in enumerate((1, 3, 2))]
    )

    def rs_copy(m, k):
        w, first, cols = CHUNKS[m]
        sems = rs_s.at[m * N_RS + k], rs_r.at[m * N_RS + k]
        if k == 11:
            piece = fin[m].at[own16]
            return remote(piece, piece, *sems, sibling)
        start, rows, dev = rs_rows[k]
        if k == 0:
            dst = rb[m]
        elif k < 7:
            dst = ra[m].at[pl.ds(64 * (k - 1), 64)]
        elif k == 7:
            dst = rx[m]
        else:
            dst = r3[m].at[pl.ds(16 * (k - 8), 16)]
        return remote(weights[w].at[pl.ds(start, rows), pl.ds(first, cols)], dst, *sems, dev)

    def rs_send(m, *ks):
        for k in ks:
            rs_copy(m, k).start()

    def rs_wait(m, *ks):
        for k in ks:
            rs_copy(m, k).wait_recv()

    def add_in(m, start, rows, source, source_row):
        w, first, cols = CHUNKS[m]
        ref = weights[w]
        width = PART // 2 if cols == PART else 512

        def body(tile):
            there = pl.ds(pl.multiple_of(tile.start + first, 128), tile.size)
            ref[pl.ds(start, rows), there] = ref[pl.ds(start, rows), there] + source[pl.ds(source_row, rows), tile]

        over(cols, width, body)

    def rs0(m):
        w, first, cols = CHUNKS[m]
        left, right = pairs[w]
        if first == 0:
            lts[w][...] = left[...].T

        def body(tile):
            there = pl.ds(pl.multiple_of(tile.start + first, 128), tile.size)
            for r in range(4):
                rows = pl.ds(256 * r, 256)
                weights[w][rows, there] = nn(lts[w][rows, :], right[:, there]).astype(BF)

        over(cols, 256, body)
        rs_send(m, 0)

    def rs1(m):
        rs_wait(m, 0)
        add_in(m, lower, HALF, rb[m], 0)
        rs_send(m, 1, 2, 3, 4)

    def rs2(m):
        rs_wait(m, 1)
        add_in(m, block[1, 0], 64, ra[m], 0)
        rs_send(m, 5)
        rs_wait(m, 2)
        add_in(m, block[3, 1], 64, ra[m], 64)
        rs_send(m, 6)

    def rs3(m):
        for k, x_ in ((3, 1), (4, 0), (5, 0), (6, 1)):
            rs_wait(m, k)
            add_in(m, block[0, x_], 64, ra[m], 64 * (k - 1))
        rs_send(m, 7)

    def rs4(m):
        rs_wait(m, 7)
        add_in(m, mine[0, 0], 64, rx[m], 0)
        rs_send(m, 8, 9, 10)

    def rs5(m):
        w, first, cols = CHUNKS[m]
        rs_wait(m, 8, 9, 10)
        total = weights[w][pl.ds(slab[0], 16), pl.ds(first, cols)].astype(F32)
        for k in range(3):
            total = total + r3[m][pl.ds(16 * k, 16), :].astype(F32)
        fin[m][own16, :] = total
        rs_send(m, 11)

    def rs6(m):
        remote(fin[m].at[own16], fin[m].at[pl.ds(pl.multiple_of(16 * (1 - c), 16), 16)],
               rs_s.at[m * N_RS + 11], rs_r.at[m * N_RS + 11], sibling).wait_recv()
        for k in range(N_RS):
            rs_copy(m, k).wait_send()

    stages = (rs0, rs1, rs2, rs3, rs4, rs5, rs6)

    def reduce(*jobs):
        for job in jobs:
            stages[job // 10](BACK_ORDER[job % 10])

    def reduce_first(*jobs):
        @pl.when(sec == 0)
        def _():
            reduce(*jobs)

    for j in range(2):
        cols = pl.ds(PART * j, PART)
        dm = nn(din[...], wd[:, cols])
        g_ = gate[:, cols]
        sg = jax.nn.sigmoid(g_)
        dgu[:, cols] = (dm * up[:, cols] * sg * (1.0 + g_ * (1.0 - sg))).astype(BF)
        dgu[:, pl.ds(FF + PART * j, PART)] = (dm * g_ * sg).astype(BF)
    reduce_first(0, 1)
    dh[...] = nt(dgu[...], wg[...])
    reduce_first(10, 2, 11, 3)
    xhat, inv = norm(h[...])
    dhv = din[...].astype(F32) + norm_back(dh[...] * gains[1:2, :], xhat, inv)
    dh[...] = dhv
    da[...] = dhv.astype(BF)
    do[...] = nn(da[...], wo[...]).astype(BF)
    reduce_first(20, 4, 12, 5)
    for hd in range(HEADS):
        dps[hd] = nt(do[:, head(hd)], value_of(hd))
    for hd in range(HEADS):
        p, dp = pf[hd], dps[hd]
        dsb[hd] = (p * (dp - jnp.sum(dp * p, axis=1, keepdims=True))).astype(BF)
    reduce_first(21, 13, 30)
    dqkv[:, QKV:] = jnp.zeros((SEQ, QKVP - QKV), BF)
    for hd in range(HEADS):
        dqkf[:, head(hd)] = nn(dsb[hd], key_of(hd)) * scale
    for g in range(KV_HEADS):
        hds = range(group * g, group * (g + 1))
        dqkf[:, head(HEADS + g)] = sum(tn(dsb[hd], qk[:, head(hd)]) for hd in hds) * scale
        dv = sum(tn(pf[hd].astype(BF), do[:, head(hd)]) for hd in hds)
        dqkv[:, QK + HEAD * g:QK + HEAD * (g + 1)] = dv.astype(BF)
    reduce_first(14, 6, 22, 31, 40)
    for t in range(QK // 128):
        cols = pl.ds(128 * t, 128)
        u = dqkf[:, cols]
        dqkv[:, cols] = (u * cosr[...] - swap(u) * sinr[...]).astype(BF)
    h[...] = nt(dqkv[...], wq[...])
    reduce_first(15, 23, 32, 41, 50)
    xhat, inv = norm(xin[...].astype(F32))
    ig[...] = (dh[...] + norm_back(h[...] * gains[0:1, :], xhat, inv)).astype(BF)

    @pl.when(sec == 1)
    def _():
        one(6).start()
        reduce(0, 1, 10, 2, 11, 3, 20, 4, 12, 5, 21, 13, 30, 14, 6, 22, 31, 40, 15, 23, 32, 41, 50)

    reduce(7, 16, 24, 33, 42, 51, 60)
    reduce(17, 25, 34, 43, 52, 61)
    a960[...] = nt(act[...], perm[...]).astype(BF)
    acts[c] = a960[own_half, :]
    one(7).start()
    i960[...] = nt(ig[...], perm[...]).astype(BF)
    igrad[c] = i960[own_half, :]
    one(8).start()
    reduce(26, 35, 44, 53, 62)
    reduce(27, 36, 45, 54, 63, 37, 46, 55, 64)

    for k in (7, 8):
        src, dst, dev = single[k]
        remote(src, (acts, igrad)[k - 7].at[1 - c], mi_s.at[k], mi_r.at[k], dev).wait_recv()
        one(k).wait_send()

    @pl.when(sec == 1)
    def _():
        one(6).wait_send()

    one(0).wait_send()
    one(1).wait_send()
    reduce(47, 56, 65)
    sum_two = sum(
        jnp.sum(fin[k][...] * pg[:, first:first + PART].astype(F32), axis=1, keepdims=True)
        for k, first in ((2, 0), (3, FF), (4, PART), (5, FF + PART))
    )
    ggf[...] = jnp.broadcast_to(sum_two, (32, 128)).T[0:1, 0:ROWS] / gf[...].astype(F32)
    reduce(57, 66)
    reduce(67)
    sum_one = jnp.sum(fin[0][:, 0:QKV] * pq[:, 0:QKV].astype(F32), axis=1, keepdims=True)
    gga[...] = jnp.broadcast_to(sum_one, (32, 128)).T[0:1, 0:ROWS] / ga[...].astype(F32)


def lay_out(*refs):
    n = len(CHUNKS)
    passed, fin, rest = refs[:4], refs[4:4 + n], refs[4 + n:]
    acts, igrad, gga, ggf, gq, go, gg, gd = rest
    for source, target in zip(passed, (acts, igrad, gga, ggf)):
        target[...] = source[...]
    targets = (gq, go, gg, gd)
    for m, (w, first, cols) in enumerate(CHUNKS):
        cols = min(cols, (QKV, D, 2 * FF, FF)[w])
        targets[w][:, 0, first:first + cols] = fin[m][0:ROWS, 0:cols]


def per_device(tokens, segments, gain_attn, w_qkv, w_out, gain_ffn, w_gu, w_down, d_out):
    n = len(CHUNKS)
    vmem = pl.BlockSpec(memory_space=pltpu.VMEM)
    per_chunk = lambda rows, kind: [pltpu.VMEM((rows, cols), kind) for _, _, cols in CHUNKS]
    scratch = (
        [pltpu.VMEM((DP, w), BF) for w in WIDTHS]
        + [pltpu.VMEM((ROWS, w), BF) for w in (QKV, D, 2 * FF, FF)]
        + [pltpu.VMEM((32, w), BF) for w in WIDTHS]
        + per_chunk(HALF, BF) + per_chunk(384, BF) + per_chunk(64, BF) + per_chunk(48, BF)
        + [pltpu.VMEM((DP, SEQ), BF)] * 4
        + [
            pltpu.VMEM((D, DP), BF),
            pltpu.VMEM((SEQ, D), BF), pltpu.VMEM((SEQ, D), BF),
            pltpu.VMEM((SEQ, DP), BF), pltpu.VMEM((SEQ, DP), BF),
            pltpu.VMEM((SEQ, DP), BF), pltpu.VMEM((SEQ, DP), BF),
            pltpu.VMEM((SEQ, D), BF), pltpu.VMEM((SEQ, D), BF),
            pltpu.VMEM((SEQ, QKVP), F32), pltpu.VMEM((SEQ, QK), BF), pltpu.VMEM((SEQ, QKVP - QK), BF),
            pltpu.VMEM((HEADS, SEQ, SEQ), F32), pltpu.VMEM((SEQ, DP), BF), pltpu.VMEM((SEQ, DP), F32),
            pltpu.VMEM((SEQ, DP), BF), pltpu.VMEM((SEQ, DP), BF),
            pltpu.VMEM((SEQ, FF), F32), pltpu.VMEM((SEQ, FF), F32), pltpu.VMEM((SEQ, FF), BF),
            pltpu.VMEM((SEQ, 2 * FF), BF), pltpu.VMEM((SEQ, DP), F32),
            pltpu.VMEM((SEQ, DP), BF), pltpu.VMEM((SEQ, DP), BF),
            pltpu.VMEM((HEADS, SEQ, SEQ), F32), pltpu.VMEM((HEADS, SEQ, SEQ), BF),
            pltpu.VMEM((SEQ, QK), F32), pltpu.VMEM((SEQ, QKVP), BF),
            pltpu.VMEM((SEQ, SEQ), F32), pltpu.VMEM((SEQ, SEQ), F32), pltpu.VMEM((8, DP), F32),
        ]
        + [pltpu.SemaphoreType.DMA((7,))]
        + [pltpu.SemaphoreType.DMA((n * N_AG,))] * 2
        + [pltpu.SemaphoreType.DMA((n * N_RS,))] * 2
        + [pltpu.SemaphoreType.DMA((9,))] * 2
    )
    shape = jax.ShapeDtypeStruct
    hbm = pl.BlockSpec(memory_space=pl.ANY)
    passed = (shape(tokens.shape, BF), shape(tokens.shape, BF), shape((1, ROWS), F32), shape((1, ROWS), F32))
    out = pl.pallas_call(
        kernel,
        out_shape=passed + tuple(shape((32, cols), F32) for _, _, cols in CHUNKS),
        in_specs=[hbm, vmem, vmem, hbm, hbm, vmem, hbm, hbm, hbm, hbm, vmem],
        out_specs=(vmem,) * (4 + n),
        scratch_shapes=scratch,
        compiler_params=pltpu.CompilerParams(
            collective_id=0, has_side_effects=True, vmem_limit_bytes=63 * 1024 * 1024
        ),
    )(
        tokens, segments, gain_attn, w_qkv[0], w_out[0], gain_ffn, w_gu[0], w_down[0], d_out,
        jnp.asarray(permutation(), BF), jnp.asarray(lane_frequencies(), F32),
    )
    acts, igrad, gga, ggf, gq, go, gg, gd = pl.pallas_call(
        lay_out,
        out_shape=passed + tuple(shape((ROWS, 1, cols), F32) for cols in (QKV, D, 2 * FF, FF)),
        in_specs=[vmem] * (4 + n),
        out_specs=(vmem,) * 8,
    )(*out)
    gq, go, gg, gd = (jnp.swapaxes(g, 0, 1) for g in (gq, go, gg, gd))
    return acts[None], igrad[None], gga, gq, go, ggf, gg, gd


def solution(mesh):
    in_specs = (
        P(None, ("fsdp", "ctx"), None),
        P(None, "fsdp"),
        P("section", "fsdp"),
        P("section", "fsdp", None),
        P("section", "fsdp", None),
        P("section", "fsdp"),
        P("section", "fsdp", None),
        P("section", "fsdp", None),
        P(None, ("fsdp", "ctx"), None),
    )
    out_specs = (
        P("section", None, ("fsdp", "ctx"), None),
        P("section", None, ("fsdp", "ctx"), None),
        P("section", "fsdp"),
        P("section", "fsdp", None),
        P("section", "fsdp", None),
        P("section", "fsdp"),
        P("section", "fsdp", None),
        P("section", "fsdp", None),
    )
    return jax.shard_map(
        per_device, mesh=mesh, in_specs=in_specs, out_specs=out_specs, check_vma=False
    )
```

time: 229 us -> 187 us (0.82)
  Pallas kernels: 218 us -> 186 us
  local copies, waits for them, and re-layouts: 10.5 us -> 0 us
    pallas_call x1 -> x2, Pallas kernels: 218 us -> 186 us  [the longest x1 183 us: per_device(): pl.pallas_call(kernel, out_shape=passed + tuple((shape((32, cols), F32) f...]
    unnamed x16 -> x0, local copies, waits for them, and re-layouts: 10.5 us -> none
where the time goes in v2:
time: 187 us
  Pallas kernels  186 us (99%)
    pallas_call x1, Pallas kernels, per_device(): pl.pallas_call(kernel, out_shape=passed + tuple((shape((32, cols), F32) f...  183 us

profile of v2, /device:TPU:1, one launch (start us, length us, event | category | flops | bytes accessed | tf_op | source)
XLA Modules:
  0.0 186.6 jit_solution(12537667333884577933)
XLA Ops:
  0.6 183.2 %shard_map.170 = (bf16[2,64,960]{2,1,0:T(8,128)(2,1)}, bf16[2,64,960]{2,1,0:T(8,128)(2,1)}, f32[1,30]{1,0:T(1,128)}, f32[1,30]{1,0:T(1,128)}, f32[32,1664]{1,0:T...) custom-call(bf16[2,64,960]{2,1,0:T(8,128)(2,1)} %tok.1, ...), custom_call_target="tpu_custom_call" | custom-call | tf_op jit(solution)/shard_map/pallas_call | solution.py:608
  183.9 2.7 %shard_map.171 = (bf16[2,64,960]{2,1,0:T(8,128)(2,1)}, bf16[2,64,960]{2,1,0:T(8,128)(2,1)}, f32[1,30]{1,0:T(1,128)}, f32[1,30]{1,0:T(1,128)}, f32[30,1,1600]{2,1...) custom-call(bf16[2,64,960]{2,1,0:T(8,128)(2,1)} %get-tuple-element.28.refs_0_, ...), custom_call_target="tpu_custom_call" | custom-call | tf_op jit(solution)/shard_map/pallas_call | solution.py:621

commit v3 on v2

--- a/solution.py
+++ b/solution.py
@@ -28,12 +28,16 @@
 MESH = pl.DeviceIdType.MESH
 
 PART = FF // 2
-CHUNKS = (
-    (0, 0, QKVP), (1, 0, DP), (2, 0, PART), (2, FF, PART), (2, PART, PART), (2, FF + PART, PART), (3, 0, PART), (3, PART, PART),
+PIECES = (
+    (0, 0, QKVP, 1), (1, 0, DP, 0), (2, 0, PART, 1), (2, FF, PART, 0), (2, PART, PART, 1), (2, FF + PART, PART, 0),
+    (3, 0, PART, 0), (3, PART, PART, 0),
+)
+SUMS = (
+    (3, 0, 640), (2, 0, PART), (2, FF, PART), (2, PART, PART), (2, FF + PART, PART), (1, 0, DP), (0, 0, QKVP),
+    (3, 640, 640), (3, PART, 640), (3, PART + 640, 640),
 )
 WIDTHS = (QKVP, DP, 2 * FF, FF)
-BACK_ORDER = (6, 7, 2, 3, 4, 5, 1, 0)
-N_AG = 18
+N_AG = 19
 N_RS = 12
 
 
@@ -80,13 +84,14 @@
     tok, seg, ga, wq_in, wo_in, gf, wg_in, wd_in, dout, perm_in, freq,
     acts, igrad, gga, ggf, *rest,
 ):
-    n = len(CHUNKS)
-    fin, rest = rest[:n], rest[n:]
+    n = len(PIECES)
+    ns = len(SUMS)
+    fin, rest = rest[:ns], rest[ns:]
     (wq, wo, wg, wd), rest = rest[:4], rest[4:]
     shards, rest = rest[:4], rest[4:]
     (pq, po, pg, pd), rest = rest[:4], rest[4:]
-    rb, ra, rx, r3 = (rest[k * n:(k + 1) * n] for k in range(4))
-    rest = rest[4 * n:]
+    rb, ra, rx, r3 = (rest[k * ns:(k + 1) * ns] for k in range(4))
+    rest = rest[4 * ns:]
     lts, rest = rest[:4], rest[4:]
     (
         perm, raw, draw, xin, din, act, ig, a960, i960,
@@ -185,9 +190,15 @@
         for key in ((0, 0), (0, 1), (3, 0), (1, 0), (3, 1), (1, 1), (2, 0), (2, 1))
     ]
 
+    ag_table.append((mine[2, 0], mine[2, 1], 64, over_x))
+    ag_parts = {
+        8: (pl.multiple_of(mine[3, 0], 32), pl.multiple_of(mine[2, 0], 32), 32, last_up),
+        9: (pl.multiple_of(mine[1, 0] + 32, 32), pl.multiple_of(mine[2, 0] + 32, 32), 32, last_down),
+    }
+
     def ag_copy(m, k, arriving=False):
-        w, first, cols = CHUNKS[m]
-        source, landing, rows, dev = ag_table[k]
+        w, first, cols, wide = PIECES[m]
+        source, landing, rows, dev = ag_parts[k] if wide and k in ag_parts else ag_table[k]
         piece = weights[w].at[pl.ds(landing if arriving else source, rows), pl.ds(first, cols)]
         return remote(piece, piece, ag_s.at[m * N_AG + k], ag_r.at[m * N_AG + k], dev)
 
@@ -209,31 +220,46 @@
         ag_wait(m, 4)
         ag_send(m, 8, 12)
         ag_wait(m, 5)
+        if PIECES[m][3]:
+            ag_send(m, 9)
         ag_send(m, 13)
 
     def ag3(m):
         ag_wait(m, 7)
-        ag_send(m, 9, 15)
+        if not PIECES[m][3]:
+            ag_send(m, 9)
+        ag_send(m, 15)
         ag_wait(m, 6)
         ag_send(m, 14)
 
     def ag4(m):
-        ag_wait(m, 8)
-        ag_send(m, 16)
-        ag_wait(m, 9)
-        ag_send(m, 17)
+        if PIECES[m][3]:
+            ag_wait(m, 8, 9)
+            ag_send(m, 18, 16)
+        else:
+            ag_wait(m, 8)
+            ag_send(m, 16)
+            ag_wait(m, 9)
+            ag_send(m, 17)
 
     def ag5(m):
+        if PIECES[m][3]:
+            ag_wait(m, 18)
+            ag_send(m, 17)
+
+    def ag6(m):
         ag_wait(m, *range(10, 18))
 
+    ag_steps = n + 6
+
     def ag_step(t):
-        for stage, late in ((ag1, 0), (ag5, 4), (ag4, 3), (ag3, 2), (ag2, 1)):
+        for stage, late in ((ag1, 0), (ag2, 2), (ag3, 3), (ag4, 4), (ag5, 5), (ag6, 6)):
             if 0 <= t - late < n:
                 stage(t - late)
 
     def ag_drain():
         for m in range(n):
-            for k in range(N_AG):
+            for k in range(N_AG if PIECES[m][3] else N_AG - 1):
                 ag_copy(m, k).wait_send()
 
     one(0).start()
@@ -247,7 +273,7 @@
             pack[:, QKV:QKV + 2] = gain_cols[0:32, 0:2].astype(BF)
         weights[w][pl.ds(slab[0], 16), :] = pack[own16, :]
         for m in range(n):
-            if CHUNKS[m][0] == w:
+            if PIECES[m][0] == w:
                 ag_send(m, 0, 1, 2)
     one(1).start()
 
@@ -289,13 +315,13 @@
 
     @pl.when(sec == 1)
     def _():
-        for t in range(1, n + 4):
+        for t in range(1, ag_steps):
             ag_step(t)
         ag_drain()
         for k in range(2, 6):
             one(k).wait_recv()
 
-    ag_first(1, 2, 3, 4)
+    ag_first(1, 2, 3, 4, 5, 6)
 
     def norm(v):
         inverse = lax.rsqrt(jnp.sum(v * v, axis=1, keepdims=True) * (1.0 / D) + EPS)
@@ -313,7 +339,7 @@
         u = qkv[:, cols]
         qk[:, cols] = (u * cosr[...] + swap(u) * sinr[...]).astype(BF)
     vv[...] = qkv[:, QK:QKVP].astype(BF)
-    ag_first(5)
+    ag_first(7)
     group = HEADS // KV_HEADS
 
     def head(hd):
@@ -332,14 +358,14 @@
         s = jnp.where(allowed, pf[hd] * scale, -1e30)
         e = jnp.exp(s - jnp.max(s, axis=1, keepdims=True))
         pf[hd] = e / jnp.sum(e, axis=1, keepdims=True)
-    ag_first(6)
+    ag_first(8)
     o[:, HEADS * HEAD:] = jnp.zeros((SEQ, DP - HEADS * HEAD), BF)
     for hd in range(HEADS):
         o[:, head(hd)] = nn(pf[hd].astype(BF), value_of(hd)).astype(BF)
     h[...] = xin[...].astype(F32) + nt(o[...], wo[...])
     xhat, _ = norm(h[...])
     xn2[...] = (xhat * gains[1:2, :]).astype(BF)
-    ag_first(7)
+    ag_first(9)
 
     def gated(j):
         cols = pl.ds(PART * j, PART)
@@ -349,11 +375,11 @@
         mm[:, cols] = (g_ * jax.nn.sigmoid(g_) * up[:, cols]).astype(BF)
 
     gated(0)
-    ag_first(8, 9)
+    ag_first(10, 11)
     gated(1)
-    ag_first(10)
+    ag_first(12)
     dh[...] = h[...] + nt(mm[:, 0:PART], wd[:, 0:PART])
-    ag_first(11)
+    ag_first(13)
     for k, cols in enumerate(own_cols):
         act[:, cols] = (dh[:, cols] + nt(mm[:, PART:], wd[cols, PART:])).astype(BF)
 
@@ -369,27 +395,25 @@
         one(6).wait_recv()
 
     pairs = ((xn1, dqkv), (da, o), (xn2, dgu), (din, mm))
-    last_at = [mod4(cc + d) for d in steps4]
-    block = {(d, x_): row(last_at[d], x_, 0) for d in steps4 for x_ in range(2)}
     lower = pl.multiple_of(c * HALF, HALF)
     upper = pl.multiple_of((1 - c) * HALF, HALF)
-    rs_rows = (
-        [(upper, HALF, sibling), (block[2, 0], 64, last_up), (block[2, 1], 64, last_down), (block[1, 1], 64, last_up),
-         (block[3, 0], 64, last_down), (block[1, 0], 64, last_up), (block[3, 1], 64, last_down), (mine[0, 1], 64, over_x)]
-        + [(slab[step], 16, first_to[k]) for k, step in enumerate((1, 3, 2))]
+    rs_table = (
+        (upper, HALF, sibling), (mine[2, 0], 64, last_up), (mine[2, 1], 64, last_down), (mine[1, 1], 64, last_up),
+        (mine[3, 0], 64, last_down), (mine[1, 0], 64, last_up), (mine[3, 1], 64, last_down), (mine[0, 1], 64, over_x),
+        (slab[1], 16, first_to[0]), (slab[3], 16, first_to[1]), (slab[2], 16, first_to[2]),
     )
 
     def rs_copy(m, k):
-        w, first, cols = CHUNKS[m]
+        w, first, cols = SUMS[m]
         sems = rs_s.at[m * N_RS + k], rs_r.at[m * N_RS + k]
         if k == 11:
             piece = fin[m].at[own16]
             return remote(piece, piece, *sems, sibling)
-        start, rows, dev = rs_rows[k]
+        start, rows, dev = rs_table[k]
         if k == 0:
             dst = rb[m]
         elif k < 7:
-            dst = ra[m].at[pl.ds(64 * (k - 1), 64)]
+            dst = ra[m].at[pl.ds(64 * (k - 1), rows)]
         elif k == 7:
             dst = rx[m]
         else:
@@ -405,9 +429,9 @@
             rs_copy(m, k).wait_recv()
 
     def add_in(m, start, rows, source, source_row):
-        w, first, cols = CHUNKS[m]
+        w, first, cols = SUMS[m]
         ref = weights[w]
-        width = PART // 2 if cols == PART else 512
+        width = 640 if cols % 640 == 0 else 512
 
         def body(tile):
             there = pl.ds(pl.multiple_of(tile.start + first, 128), tile.size)
@@ -416,7 +440,7 @@
         over(cols, width, body)
 
     def rs0(m):
-        w, first, cols = CHUNKS[m]
+        w, first, cols = SUMS[m]
         left, right = pairs[w]
         if first == 0:
             lts[w][...] = left[...].T
@@ -436,17 +460,15 @@
         rs_send(m, 1, 2, 3, 4)
 
     def rs2(m):
-        rs_wait(m, 1)
-        add_in(m, block[1, 0], 64, ra[m], 0)
-        rs_send(m, 5)
-        rs_wait(m, 2)
-        add_in(m, block[3, 1], 64, ra[m], 64)
-        rs_send(m, 6)
+        for k, into in ((1, mine[1, 0]), (2, mine[3, 1])):
+            rs_wait(m, k)
+            add_in(m, into, 64, ra[m], 64 * (k - 1))
+            rs_send(m, k + 4)
 
     def rs3(m):
-        for k, x_ in ((3, 1), (4, 0), (5, 0), (6, 1)):
+        for k, s in ((3, 1), (4, 0), (5, 0), (6, 1)):
             rs_wait(m, k)
-            add_in(m, block[0, x_], 64, ra[m], 64 * (k - 1))
+            add_in(m, mine[0, s], 64, ra[m], 64 * (k - 1))
         rs_send(m, 7)
 
     def rs4(m):
@@ -455,7 +477,7 @@
         rs_send(m, 8, 9, 10)
 
     def rs5(m):
-        w, first, cols = CHUNKS[m]
+        w, first, cols = SUMS[m]
         rs_wait(m, 8, 9, 10)
         total = weights[w][pl.ds(slab[0], 16), pl.ds(first, cols)].astype(F32)
         for k in range(3):
@@ -469,16 +491,19 @@
         for k in range(N_RS):
             rs_copy(m, k).wait_send()
 
-    stages = (rs0, rs1, rs2, rs3, rs4, rs5, rs6)
-
-    def reduce(*jobs):
-        for job in jobs:
-            stages[job // 10](BACK_ORDER[job % 10])
-
-    def reduce_first(*jobs):
+    rs_order = ((rs0, 0), (rs1, 1), (rs2, 2), (rs3, 3), (rs4, 5), (rs5, 7), (rs6, 9))
+    rs_steps = ns + 9
+
+    def reduce(*ts):
+        for t in ts:
+            for stage, late in rs_order:
+                if 0 <= t - late < ns:
+                    stage(t - late)
+
+    def reduce_first(*ts):
         @pl.when(sec == 0)
         def _():
-            reduce(*jobs)
+            reduce(*ts)
 
     for j in range(2):
         cols = pl.ds(PART * j, PART)
@@ -487,21 +512,21 @@
         sg = jax.nn.sigmoid(g_)
         dgu[:, cols] = (dm * up[:, cols] * sg * (1.0 + g_ * (1.0 - sg))).astype(BF)
         dgu[:, pl.ds(FF + PART * j, PART)] = (dm * g_ * sg).astype(BF)
-    reduce_first(0, 1)
+    reduce_first(0)
     dh[...] = nt(dgu[...], wg[...])
-    reduce_first(10, 2, 11, 3)
+    reduce_first(1)
     xhat, inv = norm(h[...])
     dhv = din[...].astype(F32) + norm_back(dh[...] * gains[1:2, :], xhat, inv)
     dh[...] = dhv
     da[...] = dhv.astype(BF)
     do[...] = nn(da[...], wo[...]).astype(BF)
-    reduce_first(20, 4, 12, 5)
+    reduce_first(2)
     for hd in range(HEADS):
         dps[hd] = nt(do[:, head(hd)], value_of(hd))
     for hd in range(HEADS):
         p, dp = pf[hd], dps[hd]
         dsb[hd] = (p * (dp - jnp.sum(dp * p, axis=1, keepdims=True))).astype(BF)
-    reduce_first(21, 13, 30)
+    reduce_first(3)
     dqkv[:, QKV:] = jnp.zeros((SEQ, QKVP - QKV), BF)
     for hd in range(HEADS):
         dqkf[:, head(hd)] = nn(dsb[hd], key_of(hd)) * scale
@@ -510,32 +535,29 @@
         dqkf[:, head(HEADS + g)] = sum(tn(dsb[hd], qk[:, head(hd)]) for hd in hds) * scale
         dv = sum(tn(pf[hd].astype(BF), do[:, head(hd)]) for hd in hds)
         dqkv[:, QK + HEAD * g:QK + HEAD * (g + 1)] = dv.astype(BF)
-    reduce_first(14, 6, 22, 31, 40)
+    reduce_first(4)
     for t in range(QK // 128):
         cols = pl.ds(128 * t, 128)
         u = dqkf[:, cols]
         dqkv[:, cols] = (u * cosr[...] - swap(u) * sinr[...]).astype(BF)
     h[...] = nt(dqkv[...], wq[...])
-    reduce_first(15, 23, 32, 41, 50)
+    reduce_first(5)
     xhat, inv = norm(xin[...].astype(F32))
     ig[...] = (dh[...] + norm_back(h[...] * gains[0:1, :], xhat, inv)).astype(BF)
 
     @pl.when(sec == 1)
     def _():
         one(6).start()
-        reduce(0, 1, 10, 2, 11, 3, 20, 4, 12, 5, 21, 13, 30, 14, 6, 22, 31, 40, 15, 23, 32, 41, 50)
-
-    reduce(7, 16, 24, 33, 42, 51, 60)
-    reduce(17, 25, 34, 43, 52, 61)
+        reduce(0, 1, 2, 3, 4, 5)
+
+    reduce(6, 7, 8, 9)
     a960[...] = nt(act[...], perm[...]).astype(BF)
     acts[c] = a960[own_half, :]
     one(7).start()
     i960[...] = nt(ig[...], perm[...]).astype(BF)
     igrad[c] = i960[own_half, :]
     one(8).start()
-    reduce(26, 35, 44, 53, 62)
-    reduce(27, 36, 45, 54, 63, 37, 46, 55, 64)
-
+    reduce(10, 11, 12)
     for k in (7, 8):
         src, dst, dev = single[k]
         remote(src, (acts, igrad)[k - 7].at[1 - c], mi_s.at[k], mi_r.at[k], dev).wait_recv()
@@ -547,39 +569,40 @@
 
     one(0).wait_send()
     one(1).wait_send()
-    reduce(47, 56, 65)
-    sum_two = sum(
-        jnp.sum(fin[k][...] * pg[:, first:first + PART].astype(F32), axis=1, keepdims=True)
-        for k, first in ((2, 0), (3, FF), (4, PART), (5, FF + PART))
-    )
-    ggf[...] = jnp.broadcast_to(sum_two, (32, 128)).T[0:1, 0:ROWS] / gf[...].astype(F32)
-    reduce(57, 66)
-    reduce(67)
-    sum_one = jnp.sum(fin[0][:, 0:QKV] * pq[:, 0:QKV].astype(F32), axis=1, keepdims=True)
-    gga[...] = jnp.broadcast_to(sum_one, (32, 128)).T[0:1, 0:ROWS] / ga[...].astype(F32)
+    reduce(*range(13, rs_steps - 2))
+
+    sums = [0.0] * 4
+    for m, (w, first, cols) in enumerate(SUMS):
+        if w in (0, 2):
+            cols = min(cols, (QKV, D, 2 * FF, FF)[w])
+            shard = (pq, po, pg, pd)[w][:, first:first + cols].astype(F32)
+            sums[w] = sums[w] + jnp.sum(fin[m][:, 0:cols] * shard, axis=1, keepdims=True)
+    gga[...] = jnp.broadcast_to(sums[0], (32, 128)).T[0:1, 0:ROWS] / ga[...].astype(F32)
+    ggf[...] = jnp.broadcast_to(sums[2], (32, 128)).T[0:1, 0:ROWS] / gf[...].astype(F32)
+    reduce(rs_steps - 2, rs_steps - 1)
 
 
 def lay_out(*refs):
-    n = len(CHUNKS)
+    n = len(SUMS)
     passed, fin, rest = refs[:4], refs[4:4 + n], refs[4 + n:]
     acts, igrad, gga, ggf, gq, go, gg, gd = rest
     for source, target in zip(passed, (acts, igrad, gga, ggf)):
         target[...] = source[...]
     targets = (gq, go, gg, gd)
-    for m, (w, first, cols) in enumerate(CHUNKS):
+    for m, (w, first, cols) in enumerate(SUMS):
         cols = min(cols, (QKV, D, 2 * FF, FF)[w])
         targets[w][:, 0, first:first + cols] = fin[m][0:ROWS, 0:cols]
 
 
 def per_device(tokens, segments, gain_attn, w_qkv, w_out, gain_ffn, w_gu, w_down, d_out):
-    n = len(CHUNKS)
+    n, ns = len(PIECES), len(SUMS)
     vmem = pl.BlockSpec(memory_space=pltpu.VMEM)
-    per_chunk = lambda rows, kind: [pltpu.VMEM((rows, cols), kind) for _, _, cols in CHUNKS]
+    per_sum = lambda rows: [pltpu.VMEM((rows, cols), BF) for _, _, cols in SUMS]
     scratch = (
         [pltpu.VMEM((DP, w), BF) for w in WIDTHS]
         + [pltpu.VMEM((ROWS, w), BF) for w in (QKV, D, 2 * FF, FF)]
         + [pltpu.VMEM((32, w), BF) for w in WIDTHS]
-        + per_chunk(HALF, BF) + per_chunk(384, BF) + per_chunk(64, BF) + per_chunk(48, BF)
+        + per_sum(HALF) + per_sum(384) + per_sum(64) + per_sum(48)
         + [pltpu.VMEM((DP, SEQ), BF)] * 4
         + [
             pltpu.VMEM((D, DP), BF),
@@ -599,7 +622,7 @@
         ]
         + [pltpu.SemaphoreType.DMA((7,))]
         + [pltpu.SemaphoreType.DMA((n * N_AG,))] * 2
-        + [pltpu.SemaphoreType.DMA((n * N_RS,))] * 2
+        + [pltpu.SemaphoreType.DMA((ns * N_RS,))] * 2
         + [pltpu.SemaphoreType.DMA((9,))] * 2
     )
     shape = jax.ShapeDtypeStruct
@@ -607,9 +630,9 @@
     passed = (shape(tokens.shape, BF), shape(tokens.shape, BF), shape((1, ROWS), F32), shape((1, ROWS), F32))
     out = pl.pallas_call(
         kernel,
-        out_shape=passed + tuple(shape((32, cols), F32) for _, _, cols in CHUNKS),
+        out_shape=passed + tuple(shape((32, cols), F32) for _, _, cols in SUMS),
         in_specs=[hbm, vmem, vmem, hbm, hbm, vmem, hbm, hbm, hbm, hbm, vmem],
-        out_specs=(vmem,) * (4 + n),
+        out_specs=(vmem,) * (4 + ns),
         scratch_shapes=scratch,
         compiler_params=pltpu.CompilerParams(
             collective_id=0, has_side_effects=True, vmem_limit_bytes=63 * 1024 * 1024
@@ -621,7 +644,7 @@
     acts, igrad, gga, ggf, gq, go, gg, gd = pl.pallas_call(
         lay_out,
         out_shape=passed + tuple(shape((ROWS, 1, cols), F32) for cols in (QKV, D, 2 * FF, FF)),
-        in_specs=[vmem] * (4 + n),
+        in_specs=[vmem] * (4 + ns),
         out_specs=(vmem,) * 8,
     )(*out)
     gq, go, gg, gd = (jnp.swapaxes(g, 0, 1) for g in (gq, go, gg, gd))

time: 187 us -> 177 us (0.947)
  Pallas kernels: 186 us -> 176 us
    pallas_call x1, Pallas kernels: 183 us -> 174 us  [per_device(): pl.pallas_call(kernel, out_shape=passed + tuple((shape((32, cols), F32) f...]
where the time goes in v3:
time: 177 us
  Pallas kernels  176 us (99%)
    pallas_call x1, Pallas kernels, per_device(): pl.pallas_call(kernel, out_shape=passed + tuple((shape((32, cols), F32) f...  174 us

profile of v3, /device:TPU:1, one launch (start us, length us, event | category | flops | bytes accessed | tf_op | source)
XLA Modules:
  0.0 177.2 jit_solution(5207177287884948825)
XLA Ops:
  0.6 173.7 %shard_map.170 = (bf16[2,64,960]{2,1,0:T(8,128)(2,1)}, bf16[2,64,960]{2,1,0:T(8,128)(2,1)}, f32[1,30]{1,0:T(1,128)}, f32[1,30]{1,0:T(1,128)}, f32[32,640]{1,0:T(...) custom-call(bf16[2,64,960]{2,1,0:T(8,128)(2,1)} %tok.1, ...), custom_call_target="tpu_custom_call" | custom-call | tf_op jit(solution)/shard_map/pallas_call | solution.py:631
  174.4 2.7 %shard_map.171 = (bf16[2,64,960]{2,1,0:T(8,128)(2,1)}, bf16[2,64,960]{2,1,0:T(8,128)(2,1)}, f32[1,30]{1,0:T(1,128)}, f32[1,30]{1,0:T(1,128)}, f32[30,1,1600]{2,1...) custom-call(bf16[2,64,960]{2,1,0:T(8,128)(2,1)} %get-tuple-element.30.refs_0_, ...), custom_call_target="tpu_custom_call" | custom-call | tf_op jit(solution)/shard_map/pallas_call | solution.py:644

commit v4 on v3

--- a/solution.py
+++ b/solution.py
@@ -33,12 +33,12 @@
     (3, 0, PART, 0), (3, PART, PART, 0),
 )
 SUMS = (
-    (3, 0, 640), (2, 0, PART), (2, FF, PART), (2, PART, PART), (2, FF + PART, PART), (1, 0, DP), (0, 0, QKVP),
-    (3, 640, 640), (3, PART, 640), (3, PART + 640, 640),
+    (3, 0, 640), (3, 640, 640), (2, 0, PART), (2, FF, PART), (2, PART, PART), (2, FF + PART, PART), (1, 0, DP), (0, 0, QKVP),
+    (3, PART, 640), (3, PART + 640, 640),
 )
 WIDTHS = (QKVP, DP, 2 * FF, FF)
 N_AG = 19
-N_RS = 12
+N_RS = 16
 
 
 def permutation():
@@ -141,9 +141,11 @@
     last_up, last_down = at(a, x, mod4(cc + 1)), at(a, x, mod4(cc + 3))
     over_x = at(a, other_x, cc)
     first_to = [at(mod4(a + step), x, cc) for step in (1, 3, 2)]
+    last_far = at(a, x, mod4(cc + 2))
+    across = [at(mod4(a + step), other_x, cc) for step in range(4)]
 
     barrier = pltpu.get_barrier_semaphore()
-    friends = first_to + [over_x, last_up, last_down, sibling, partner]
+    friends = first_to + across + [last_up, last_down, last_far, sibling, partner]
     for dev in friends:
         pl.semaphore_signal(barrier, inc=1, device_id=dev, device_id_type=MESH)
 
@@ -400,8 +402,8 @@
     rs_table = (
         (upper, HALF, sibling), (mine[2, 0], 64, last_up), (mine[2, 1], 64, last_down), (mine[1, 1], 64, last_up),
         (mine[3, 0], 64, last_down), (mine[1, 0], 64, last_up), (mine[3, 1], 64, last_down), (mine[0, 1], 64, over_x),
-        (slab[1], 16, first_to[0]), (slab[3], 16, first_to[1]), (slab[2], 16, first_to[2]),
-    )
+        (slab[1], 16, first_to[0]), (slab[3], 16, first_to[1]), (slab[2], 16, first_to[2]), None,
+    ) + tuple((row(cc, other_x, mod4(a + step)), 16, across[step]) for step in steps4)
 
     def rs_copy(m, k):
         w, first, cols = SUMS[m]
@@ -410,12 +412,16 @@
             piece = fin[m].at[own16]
             return remote(piece, piece, *sems, sibling)
         start, rows, dev = rs_table[k]
+        if m == ns - 1 and k in (1, 2):
+            dev = last_far
         if k == 0:
             dst = rb[m]
         elif k < 7:
             dst = ra[m].at[pl.ds(64 * (k - 1), rows)]
         elif k == 7:
             dst = rx[m]
+        elif k > 11:
+            dst = rx[m].at[pl.ds(16 * (k - 12), 16)]
         else:
             dst = r3[m].at[pl.ds(16 * (k - 8), 16)]
         return remote(weights[w].at[pl.ds(start, rows), pl.ds(first, cols)], dst, *sems, dev)
@@ -458,8 +464,12 @@
         rs_wait(m, 0)
         add_in(m, lower, HALF, rb[m], 0)
         rs_send(m, 1, 2, 3, 4)
+        if m == ns - 1:
+            rs_send(m, 5, 6)
 
     def rs2(m):
+        if m == ns - 1:
+            return
         for k, into in ((1, mine[1, 0]), (2, mine[3, 1])):
             rs_wait(m, k)
             add_in(m, into, 64, ra[m], 64 * (k - 1))
@@ -469,9 +479,17 @@
         for k, s in ((3, 1), (4, 0), (5, 0), (6, 1)):
             rs_wait(m, k)
             add_in(m, mine[0, s], 64, ra[m], 64 * (k - 1))
-        rs_send(m, 7)
+        if m == ns - 1:
+            for k in (1, 2):
+                rs_wait(m, k)
+                add_in(m, mine[0, k - 1], 64, ra[m], 64 * (k - 1))
+            rs_send(m, 12, 13, 14, 15, 8, 9, 10)
+        else:
+            rs_send(m, 7)
 
     def rs4(m):
+        if m == ns - 1:
+            return
         rs_wait(m, 7)
         add_in(m, mine[0, 0], 64, rx[m], 0)
         rs_send(m, 8, 9, 10)
@@ -482,13 +500,17 @@
         total = weights[w][pl.ds(slab[0], 16), pl.ds(first, cols)].astype(F32)
         for k in range(3):
             total = total + r3[m][pl.ds(16 * k, 16), :].astype(F32)
+        if m == ns - 1:
+            rs_wait(m, 12, 13, 14, 15)
+            for k in steps4:
+                total = total + rx[m][pl.ds(16 * k, 16), :].astype(F32)
         fin[m][own16, :] = total
         rs_send(m, 11)
 
     def rs6(m):
         remote(fin[m].at[own16], fin[m].at[pl.ds(pl.multiple_of(16 * (1 - c), 16), 16)],
                rs_s.at[m * N_RS + 11], rs_r.at[m * N_RS + 11], sibling).wait_recv()
-        for k in range(N_RS):
+        for k in range(12) if m < ns - 1 else (*range(7), *range(8, 16)):
             rs_copy(m, k).wait_send()
 
     rs_order = ((rs0, 0), (rs1, 1), (rs2, 2), (rs3, 3), (rs4, 5), (rs5, 7), (rs6, 9))
@@ -497,8 +519,16 @@
     def reduce(*ts):
         for t in ts:
             for stage, late in rs_order:
-                if 0 <= t - late < ns:
+                if 0 <= t - late < ns and not (late < 2 and t - late < 2):
                     stage(t - late)
+
+    def reduce_start():
+        rs0(0)
+        rs0(1)
+
+    def reduce_links():
+        rs1(0)
+        rs1(1)
 
     def reduce_first(*ts):
         @pl.when(sec == 0)
@@ -512,21 +542,25 @@
         sg = jax.nn.sigmoid(g_)
         dgu[:, cols] = (dm * up[:, cols] * sg * (1.0 + g_ * (1.0 - sg))).astype(BF)
         dgu[:, pl.ds(FF + PART * j, PART)] = (dm * g_ * sg).astype(BF)
-    reduce_first(0)
-    dh[...] = nt(dgu[...], wg[...])
-    reduce_first(1)
+    pl.when(sec == 0)(reduce_start)
+    for cols in own_cols[:2]:
+        dh[:, cols] = nt(dgu[...], wg[cols, :])
+    pl.when(sec == 0)(reduce_links)
+    for cols in own_cols[2:]:
+        dh[:, cols] = nt(dgu[...], wg[cols, :])
+    reduce_first(2)
     xhat, inv = norm(h[...])
     dhv = din[...].astype(F32) + norm_back(dh[...] * gains[1:2, :], xhat, inv)
     dh[...] = dhv
     da[...] = dhv.astype(BF)
     do[...] = nn(da[...], wo[...]).astype(BF)
-    reduce_first(2)
+    reduce_first(3)
     for hd in range(HEADS):
         dps[hd] = nt(do[:, head(hd)], value_of(hd))
     for hd in range(HEADS):
         p, dp = pf[hd], dps[hd]
         dsb[hd] = (p * (dp - jnp.sum(dp * p, axis=1, keepdims=True))).astype(BF)
-    reduce_first(3)
+    reduce_first(4)
     dqkv[:, QKV:] = jnp.zeros((SEQ, QKVP - QKV), BF)
     for hd in range(HEADS):
         dqkf[:, head(hd)] = nn(dsb[hd], key_of(hd)) * scale
@@ -535,22 +569,24 @@
         dqkf[:, head(HEADS + g)] = sum(tn(dsb[hd], qk[:, head(hd)]) for hd in hds) * scale
         dv = sum(tn(pf[hd].astype(BF), do[:, head(hd)]) for hd in hds)
         dqkv[:, QK + HEAD * g:QK + HEAD * (g + 1)] = dv.astype(BF)
-    reduce_first(4)
+    reduce_first(5)
     for t in range(QK // 128):
         cols = pl.ds(128 * t, 128)
         u = dqkf[:, cols]
         dqkv[:, cols] = (u * cosr[...] - swap(u) * sinr[...]).astype(BF)
     h[...] = nt(dqkv[...], wq[...])
-    reduce_first(5)
+    reduce_first(6)
     xhat, inv = norm(xin[...].astype(F32))
     ig[...] = (dh[...] + norm_back(h[...] * gains[0:1, :], xhat, inv)).astype(BF)
 
     @pl.when(sec == 1)
     def _():
         one(6).start()
-        reduce(0, 1, 2, 3, 4, 5)
-
-    reduce(6, 7, 8, 9)
+        reduce_start()
+        reduce_links()
+        reduce(2, 3, 4, 5, 6)
+
+    reduce(7, 8, 9)
     a960[...] = nt(act[...], perm[...]).astype(BF)
     acts[c] = a960[own_half, :]
     one(7).start()

time: 177 us -> 176 us (level)
  no operation moved by 1% of the time
where the time goes in v4:
time: 176 us
  Pallas kernels  175 us (99%)
    pallas_call x1, Pallas kernels, per_device(): pl.pallas_call(kernel, out_shape=passed + tuple((shape((32, cols), F32) f...  172 us

profile of v4, /device:TPU:1, one launch (start us, length us, event | category | flops | bytes accessed | tf_op | source)
XLA Modules:
  0.0 175.6 jit_solution(909632458247700789)
XLA Ops:
  0.6 172.1 %shard_map.170 = (bf16[2,64,960]{2,1,0:T(8,128)(2,1)}, bf16[2,64,960]{2,1,0:T(8,128)(2,1)}, f32[1,30]{1,0:T(1,128)}, f32[1,30]{1,0:T(1,128)}, f32[32,640]{1,0:T(...) custom-call(bf16[2,64,960]{2,1,0:T(8,128)(2,1)} %tok.1, ...), custom_call_target="tpu_custom_call" | custom-call | tf_op jit(solution)/shard_map/pallas_call | solution.py:667
  172.8 2.7 %shard_map.171 = (bf16[2,64,960]{2,1,0:T(8,128)(2,1)}, bf16[2,64,960]{2,1,0:T(8,128)(2,1)}, f32[1,30]{1,0:T(1,128)}, f32[1,30]{1,0:T(1,128)}, f32[30,1,1600]{2,1...) custom-call(bf16[2,64,960]{2,1,0:T(8,128)(2,1)} %get-tuple-element.30.refs_0_, ...), custom_call_target="tpu_custom_call" | custom-call | tf_op jit(solution)/shard_map/pallas_call | solution.py:680

commit v5 on v4

--- a/solution.py
+++ b/solution.py
@@ -29,7 +29,7 @@
 
 PART = FF // 2
 PIECES = (
-    (0, 0, QKVP, 1), (1, 0, DP, 0), (2, 0, PART, 1), (2, FF, PART, 0), (2, PART, PART, 1), (2, FF + PART, PART, 0),
+    (0, 0, QKVP, 1), (1, 0, DP, 0), (2, 0, PART, 0), (2, FF, PART, 1), (2, PART, PART, 0), (2, FF + PART, PART, 1),
     (3, 0, PART, 0), (3, PART, PART, 0),
 )
 SUMS = (
@@ -309,6 +309,9 @@
     def _():
         din[...] = nn(draw[...], perm[...]).astype(BF)
 
+    def read_gains():
+        gains[...] = wq[:, 1536:1664].astype(F32).T[64:72, :]
+
     def ag_first(*ts):
         @pl.when(sec == 0)
         def _():
@@ -320,10 +323,12 @@
         for t in range(1, ag_steps):
             ag_step(t)
         ag_drain()
+        read_gains()
         for k in range(2, 6):
             one(k).wait_recv()
 
     ag_first(1, 2, 3, 4, 5, 6)
+    pl.when(sec == 0)(read_gains)
 
     def norm(v):
         inverse = lax.rsqrt(jnp.sum(v * v, axis=1, keepdims=True) * (1.0 / D) + EPS)
@@ -332,7 +337,6 @@
     def norm_back(d, normal, inverse):
         return inverse * (d - normal * (jnp.sum(normal * d, axis=1, keepdims=True) * (1.0 / D)))
 
-    gains[...] = wq[:, 1536:1664].astype(F32).T[64:72, :]
     xhat, _ = norm(xin[...].astype(F32))
     xn1[...] = (xhat * gains[0:1, :]).astype(BF)
     qkv[...] = nn(xn1[...], wq[...])
@@ -513,7 +517,7 @@
         for k in range(12) if m < ns - 1 else (*range(7), *range(8, 16)):
             rs_copy(m, k).wait_send()
 
-    rs_order = ((rs0, 0), (rs1, 1), (rs2, 2), (rs3, 3), (rs4, 5), (rs5, 7), (rs6, 9))
+    rs_order = ((rs1, 1), (rs0, 0), (rs2, 2), (rs3, 3), (rs4, 5), (rs5, 7), (rs6, 9))
     rs_steps = ns + 9
 
     def reduce(*ts):

time: 176 us -> 174 us (0.989)
  Pallas kernels: 175 us -> 173 us
    pallas_call x1, Pallas kernels: 172 us -> 170 us  [per_device(): pl.pallas_call(kernel, out_shape=passed + tuple((shape((32, cols), F32) f...]
where the time goes in v5:
time: 174 us
  Pallas kernels  173 us (99%)
    pallas_call x1, Pallas kernels, per_device(): pl.pallas_call(kernel, out_shape=passed + tuple((shape((32, cols), F32) f...  170 us

profile of v5, /device:TPU:1, one launch (start us, length us, event | category | flops | bytes accessed | tf_op | source)
XLA Modules:
  0.0 173.8 jit_solution(17760346222905899938)
XLA Ops:
  0.6 170.3 %shard_map.170 = (bf16[2,64,960]{2,1,0:T(8,128)(2,1)}, bf16[2,64,960]{2,1,0:T(8,128)(2,1)}, f32[1,30]{1,0:T(1,128)}, f32[1,30]{1,0:T(1,128)}, f32[32,640]{1,0:T(...) custom-call(bf16[2,64,960]{2,1,0:T(8,128)(2,1)} %tok.1, ...), custom_call_target="tpu_custom_call" | custom-call | tf_op jit(solution)/shard_map/pallas_call | solution.py:671
  170.9 2.7 %shard_map.171 = (bf16[2,64,960]{2,1,0:T(8,128)(2,1)}, bf16[2,64,960]{2,1,0:T(8,128)(2,1)}, f32[1,30]{1,0:T(1,128)}, f32[1,30]{1,0:T(1,128)}, f32[30,1,1600]{2,1...) custom-call(bf16[2,64,960]{2,1,0:T(8,128)(2,1)} %get-tuple-element.30.refs_0_, ...), custom_call_target="tpu_custom_call" | custom-call | tf_op jit(solution)/shard_map/pallas_call | solution.py:684
